TPU v7x, 32 devices: a whole 2x2x4 slice. The times are simulated.
32 devices in a mesh: row: 4 (over x, core), col: 8 (over z, y).
Axes of the slice: x: 2, y: 2, z: 4, core: 2. Of those that a mesh axis runs over, the one named last changes fastest.
Arguments:
- tokens: bfloat16 [24576, 768], P(('row', 'col')), may hold values from -6 to 6
- w_qkv: bfloat16 [3, 768, 768], replicated, may hold values from -0.21875 to 0.21875
- w_attn_out: bfloat16 [768, 768], replicated, may hold values from -0.875 to 0.875
- w_in: bfloat16 [768, 3072], replicated, may hold values from -0.21875 to 0.21875
- w_out: bfloat16 [3072, 768], replicated, may hold values from -0.109375 to 0.109375
- vectors: float32 [9216], replicated
- out_grad: bfloat16 [24576, 768], P(('row', 'col')), may hold values from -6 to 6
- span_count: int32 [32], replicated, may hold values from 1 to 6, as said below
- pair_index: int32 [192], replicated, may hold values from 0 to 191, as said below
- owner_list: int32 [48], replicated, may hold values from 0 to 47, each once
- master: float32 [48, 768, 192], P('col'), may hold values from -0.21875 to 0.21875
- first_moment: float32 [48, 768, 192], P('col'), may hold values from -56 to 56
- second_moment: float32 [48, 768, 192], P('col'), may hold values from 6.144 to 24.576
- left_basis: float32 [48, 768, 768], P('col'), as said below
- right_basis: float32 [48, 192, 192], P('col'), as said below
- vec_first: float32 [9216], replicated, may hold values from -112 to 112
- vec_second: float32 [9216], replicated, may hold values from 24.576 to 98.304
Outputs:
- encoded: bfloat16 [24576, 768], P(('row', 'col'))
- input_grad: float32 [24576, 768], P(('row', 'col'))
- loss: float32 [], replicated
- new_master: float32 [48, 768, 192], P('col')
- new_first: float32 [48, 768, 192], P('col')
- new_second: float32 [48, 768, 192], P('col')
- master_copy: bfloat16 [48, 768, 192], P('col')
- vec_new: float32 [9216], replicated
- vec_first_new: float32 [9216], replicated
- vec_second_new: float32 [9216], replicated
Inputs may be any that keep to these rules, and one draw needn't show every extreme that they name: `span_count`: the live spans of a device fill its first slots; the last device has 6 live spans. pair_index[i] = i for padding slots and for live spans without a partner; otherwise j = pair_index[i] is another live span, on any device, with pair_index[j] = i. `owner_list`: each block number once. `left_basis`: each [s] is orthogonal: the columns are orthonormal DCT-II basis vectors, permuted and signed. `right_basis`: each [s] is orthogonal: the columns are orthonormal DCT-II basis vectors, permuted and signed.
All inputs are finite; a program needn't handle non-finite values.
Results may differ from a plain program's by a relative error of at most 0.01.
Values may be sent and summed in bfloat16 or wider, within the bound.
No kernel may reach another device: no remote copies, remote signals or barrier semaphores. Data moves between devices by JAX's collectives and lax.ppermute only.
A program may use at most 192 MiB of HBM per device.

v0:
```python
from functools import partial

import jax
import jax.numpy as jnp
from jax import lax
from jax.experimental import pallas as pl
from jax.experimental.pallas import tpu as pltpu
from jax.sharding import PartitionSpec as P

D = 768
HEADS = 12
HEAD = 64
FF = 3072
SPAN = 128
STEP = 10
GROUP = 8

RATE = 0.01
DECAY = 0.01
VECTOR_RATE = 0.3

LOW = jnp.bfloat16
F32 = jnp.float32
TALL = 2 * SPAN
VMEM_LIMIT = 56 * 1024 * 1024


def dot(left_side, right_side, contract=(1, 0)):
    dims = (((contract[0],), (contract[1],)), ((), ()))
    return lax.dot_general(left_side, right_side, dims, preferred_element_type=F32)


def whole(shape):
    return pl.BlockSpec(shape, lambda *ids: (0,) * len(shape))


def params():
    return pltpu.CompilerParams(vmem_limit_bytes=VMEM_LIMIT)


def row_of(rows, index):
    return rows[:, index * D : (index + 1) * D]


def live_rows(place, counts, first_row, height):
    at = first_row + lax.broadcasted_iota(jnp.int32, (height, 1), 0)
    return jnp.where(at < counts[place[0]] * SPAN, 1.0, 0.0)


ANY = pl.BlockSpec(memory_space=pl.ANY)
SMEM = pl.BlockSpec(memory_space=pltpu.SMEM)


def split_heads(pair):
    lane = lax.broadcasted_iota(jnp.int32, pair.shape, 1)
    zero = jnp.zeros_like(pair)
    return jnp.concatenate([jnp.where(lane < HEAD, pair, zero), jnp.where(lane < HEAD, zero, pair)])


def normalise(scores):
    peak = jnp.max(scores, axis=-1, keepdims=True)
    raised = jnp.exp(scores - peak)
    return raised * (1.0 / jnp.sum(raised, axis=-1, keepdims=True))


def attend_kernel(tokens, w_qkv, rows, q_out, k_out, v_out, p_out, a_out):
    block = tokens[...]
    scaling = HEAD ** (-0.5)
    q_out[...] = ((dot(block, w_qkv[0]) + row_of(rows, 4)).astype(LOW) * scaling).astype(LOW)
    k_out[...] = dot(block, w_qkv[1]).astype(LOW)
    v_out[...] = (dot(block, w_qkv[2]) + row_of(rows, 5)).astype(LOW)
    for span in range(TALL // SPAN):
        at = slice(span * SPAN, (span + 1) * SPAN)
        for pair in range(HEADS // 2):
            lanes = slice(pair * 2 * HEAD, (pair + 1) * 2 * HEAD)
            scores = dot(q_out[at, lanes], split_heads(k_out[at, lanes]), (1, 1))
            weights = jnp.concatenate(
                [normalise(scores[:, :SPAN]), normalise(scores[:, SPAN:])], axis=1
            ).astype(LOW)
            p_out[span, pair] = weights
            a_out[at, lanes] = dot(weights, split_heads(v_out[at, lanes])).astype(LOW)


def attend(tokens, w_qkv, rows):
    total = tokens.shape[0]
    tall = pl.BlockSpec((TALL, D), lambda i: (i, 0))
    like = jax.ShapeDtypeStruct((total, D), LOW)
    spans = TALL // SPAN
    return pl.pallas_call(
        attend_kernel,
        grid=(total // TALL,),
        in_specs=[tall, whole(w_qkv.shape), whole(rows.shape)],
        out_specs=[
            tall,
            tall,
            tall,
            pl.BlockSpec((spans, HEADS // 2, SPAN, 2 * SPAN), lambda i: (i, 0, 0, 0)),
            tall,
        ],
        out_shape=[
            like,
            like,
            like,
            jax.ShapeDtypeStruct((total // SPAN, HEADS // 2, SPAN, 2 * SPAN), LOW),
            like,
        ],
        compiler_params=params(),
        cost_estimate=pl.CostEstimate(
            flops=2 * total * D * (3 * D + 2 * SPAN),
            bytes_accessed=14 * total * D + 6 * D * D,
            transcendentals=total * HEADS * SPAN,
        ),
        name="attend",
    )(tokens, w_qkv, rows)


def unit_norm(resid):
    centred = resid - jnp.mean(resid, axis=-1, keepdims=True)
    inverse = lax.rsqrt(jnp.mean(centred * centred, axis=-1, keepdims=True) + 1e-06)
    return centred * inverse, inverse


def gelu_pair(x):
    z = jnp.abs(x) * 0.7071067811865476
    base = 1.0 + 0.3275911 * z
    t = pltpu.reciprocal(base, approx=True)
    t = t * (2.0 - base * t)
    poly = 0.5 * 1.061405429
    for term in (-1.453152027, 1.421413741, -0.284496736, 0.254829592):
        poly = poly * t + 0.5 * term
    gauss = jnp.exp(-(z * z))
    tail = poly * t * gauss
    cdf = jnp.where(x < 0, tail, 1.0 - tail)
    return x * cdf, cdf + x * gauss * 0.3989422804014327


def feed_kernel(
    place, counts, tokens, attended, w_attn, w_in, w_out, rows,
    enc_out, hid_out, slope_out, norm_out, u1_out, i1_out, u2_out, i2_out,
):
    resid = tokens[...].astype(F32) + dot(attended[...], w_attn[...]) + row_of(rows, 6)
    unit_one, inverse_one = unit_norm(resid)
    normed = unit_one * row_of(rows, 0) + row_of(rows, 2)
    u1_out[...] = unit_one.astype(LOW)
    i1_out[...] = inverse_one
    norm_out[...] = normed.astype(LOW)
    step = 256
    for at in range(0, FF, step):
        bias = rows[:, 8 * D + at : 8 * D + at + step]
        pre_act = dot(norm_out[...], w_in[:, at : at + step]) + bias
        hidden, slope = gelu_pair(pre_act)
        hid_out[:, at : at + step] = hidden.astype(LOW)
        slope_out[:, at : at + step] = slope.astype(LOW)
    resid = normed + dot(hid_out[...], w_out[...]) + row_of(rows, 7)
    unit_two, inverse_two = unit_norm(resid)
    u2_out[...] = unit_two.astype(LOW)
    i2_out[...] = inverse_two
    live = live_rows(place, counts, pl.program_id(0) * TALL, TALL)
    enc_out[...] = (live * (unit_two * row_of(rows, 1) + row_of(rows, 3))).astype(LOW)


def feed(place, counts, tokens, attended, w_attn, w_in, w_out, rows):
    total = tokens.shape[0]
    tall = lambda width: pl.BlockSpec((TALL, width), lambda i: (i, 0))
    like = lambda width, kind: jax.ShapeDtypeStruct((total, width), kind)
    return pl.pallas_call(
        feed_kernel,
        grid=(total // TALL,),
        in_specs=[SMEM, SMEM, tall(D), tall(D)]
        + [whole(a.shape) for a in (w_attn, w_in, w_out, rows)],
        out_specs=[tall(D), tall(FF), tall(FF), tall(D), tall(D), tall(1), tall(D), tall(1)],
        out_shape=[
            like(D, LOW), like(FF, LOW), like(FF, LOW), like(D, LOW),
            like(D, LOW), like(1, F32), like(D, LOW), like(1, F32),
        ],
        compiler_params=params(),
        cost_estimate=pl.CostEstimate(
            flops=2 * total * D * (D + 2 * FF),
            bytes_accessed=total * (12 * D + 4 * FF) + 4 * D * FF,
            transcendentals=total * FF * 2,
        ),
        name="feed",
    )(place, counts, tokens, attended, w_attn, w_in, w_out, rows)


def norm_back(grad_out, unit_rows, inverse, gain):
    scaled = grad_out * gain
    along = jnp.mean(scaled * unit_rows, axis=-1, keepdims=True)
    return inverse * (scaled - jnp.mean(scaled, axis=-1, keepdims=True) - unit_rows * along)


def column_sums(*arrays):
    return [jnp.sum(a, axis=0, keepdims=True) for a in arrays]


def outer_kernel(place, counts, out_grad, grad_cls, unit_two, inverse_two, rows, two_out, low_out, vec_out):
    spot = lax.broadcasted_iota(jnp.int32, (SPAN, 1), 0) == 0
    sums = None
    for span in range(out_grad.shape[0] // SPAN):
        at = slice(span * SPAN, (span + 1) * SPAN)
        added = jnp.where(spot, grad_cls[span : span + 1], 0.0)
        live = live_rows(place, counts, span * SPAN, SPAN)
        grad_y = live * (out_grad[at].astype(F32) + added)
        unit_rows = unit_two[at].astype(F32)
        grad_two = norm_back(grad_y, unit_rows, inverse_two[at], row_of(rows, 1))
        two_out[at] = grad_two
        low_out[at] = grad_two.astype(LOW)
        here = column_sums(grad_y * unit_rows, grad_y, grad_two)
        sums = here if sums is None else [a + b for a, b in zip(sums, here)]
    for index, total in enumerate(sums):
        vec_out[index : index + 1] = total


def outer_grad(place, counts, out_grad, grad_cls, unit_two, inverse_two, rows):
    total = out_grad.shape[0]
    return pl.pallas_call(
        outer_kernel,
        in_specs=[SMEM, SMEM] + [pl.BlockSpec(memory_space=pltpu.VMEM)] * 5,
        out_shape=[
            jax.ShapeDtypeStruct((total, D), F32),
            jax.ShapeDtypeStruct((total, D), LOW),
            jax.ShapeDtypeStruct((3, D), F32),
        ],
        compiler_params=params(),
        cost_estimate=pl.CostEstimate(
            flops=20 * total * D, bytes_accessed=10 * total * D, transcendentals=0
        ),
        name="outer",
    )(place, counts, out_grad, grad_cls, unit_two, inverse_two, rows)


def weight_kernel(panels, ordered_after, bit, *refs):
    left_side, right_side, *rest = refs[ordered_after:]
    extra_left, extra_right = rest[:-2] or (None, None)
    send_out, keep_out = rest[-2:]

    def store(left_from, right_from):
        value = dot(left_from[...], right_from[...], (0, 0)).astype(LOW)

        @pl.when(pl.program_id(0) == 0)
        def _():
            send_out[0] = value

        @pl.when(pl.program_id(0) == 1)
        def _():
            keep_out[0] = value

    if extra_left is None:
        store(left_side, right_side)
        return

    @pl.when(pl.program_id(1) < panels)
    def _():
        store(left_side, right_side)

    @pl.when(pl.program_id(1) == panels)
    def _():
        store(extra_left, extra_right)


def weight_grad(after, bit, left_side, right_side, panels, banded, extra=()):
    total = left_side.shape[0]
    half = D // 2
    every = panels + len(extra) // 2

    def side_of(phase, bit):
        return jnp.where(phase == 0, 1 - bit[0], bit[0])

    def left_at(phase, panel, bit):
        side = side_of(phase, bit)
        return (0, jnp.minimum(panel, panels - 1) * 2 + side if banded else side)

    def right_at(phase, panel, bit):
        return (0, 0 if banded else jnp.minimum(panel, panels - 1))

    like = jax.ShapeDtypeStruct((every, half, D), LOW)
    tall = lambda width, at: pl.BlockSpec((total, width), at)
    more = [tall(half, lambda f, p, b: (0, side_of(f, b))), tall(D, lambda f, p, b: (0, 0))]
    return pl.pallas_call(
        partial(weight_kernel, panels, len(after)),
        grid_spec=pltpu.PrefetchScalarGridSpec(
            num_scalar_prefetch=1,
            grid=(2, every),
            in_specs=[ANY] * len(after)
            + [tall(half, left_at), tall(D, right_at)]
            + more[: len(extra)],
            out_specs=[
                pl.BlockSpec((1, half, D), lambda f, p, b: (jnp.where(f == 0, p, every - 1), 0, 0)),
                pl.BlockSpec((1, half, D), lambda f, p, b: (jnp.where(f == 0, 0, p), 0, 0)),
            ],
        ),
        out_shape=[like, like],
        compiler_params=params(),
        cost_estimate=pl.CostEstimate(
            flops=2 * total * D * D * every,
            bytes_accessed=2 * (total + D) * D * every,
            transcendentals=0,
        ),
        name="weight",
    )(bit.reshape(1), *after, left_side, right_side, *extra)


def slope_kernel(*refs):
    low, slope, w_out, pre_out, vec_out = refs[-5:]
    step = 256
    for at in range(0, pre_out.shape[1], step):
        here = slice(at, at + step)
        grad_pre = dot(low[...], w_out[here], (1, 1)) * slope[:, here].astype(F32)
        pre_out[:, here] = grad_pre.astype(LOW)
        vec_out[0, :, here] = jnp.sum(grad_pre, axis=0, keepdims=True)


def slope_grad(after, low, slope, w_out):
    total = low.shape[0]
    band = pl.BlockSpec((total, D), lambda i: (0, i))
    return pl.pallas_call(
        slope_kernel,
        grid=(FF // D,),
        in_specs=[ANY] * len(after)
        + [whole(low.shape), band, pl.BlockSpec((D, D), lambda i: (i, 0))],
        out_specs=[band, pl.BlockSpec((1, 1, D), lambda i: (i, 0, 0))],
        out_shape=[
            jax.ShapeDtypeStruct((total, FF), LOW),
            jax.ShapeDtypeStruct((FF // D, 1, D), F32),
        ],
        compiler_params=params(),
        cost_estimate=pl.CostEstimate(
            flops=2 * total * D * FF, bytes_accessed=4 * total * FF + 2 * D * FF, transcendentals=0
        ),
        name="slope",
    )(*after, low, slope, w_out)


def inner_kernel(*refs):
    pre_low, grad_two, unit_one, inverse_one, w_attn, w_in, rows = refs[-11:-4]
    one_out, mixed_out, ga_out, vec_out = refs[-4:]
    first = pl.program_id(0) == 0

    @pl.when(first)
    def _():
        vec_out[...] = jnp.zeros_like(vec_out)

    grad_normed = grad_two[...] + dot(pre_low[...], w_in[...], (1, 1))
    unit_rows = unit_one[...].astype(F32)
    grad_one = norm_back(grad_normed, unit_rows, inverse_one[...], row_of(rows, 0))
    one_out[...] = grad_one
    mixed = grad_one.astype(LOW)
    mixed_out[...] = mixed
    ga_out[...] = dot(mixed, w_attn[...], (1, 1)).astype(LOW)
    for index, total in enumerate(column_sums(grad_normed * unit_rows, grad_normed, grad_one)):
        vec_out[index : index + 1] += total


def inner_grad(after, pre_low, grad_two, unit_one, inverse_one, w_attn, w_in, rows):
    total = pre_low.shape[0]
    tall = lambda width: pl.BlockSpec((TALL, width), lambda i: (i, 0))
    like = lambda width, kind: jax.ShapeDtypeStruct((total, width), kind)
    return pl.pallas_call(
        inner_kernel,
        grid=(total // TALL,),
        in_specs=[ANY] * len(after)
        + [tall(FF), tall(D), tall(D), tall(1)]
        + [whole(a.shape) for a in (w_attn, w_in, rows)],
        out_specs=[tall(D), tall(D), tall(D), whole((3, D))],
        out_shape=[
            like(D, F32), like(D, LOW), like(D, LOW), jax.ShapeDtypeStruct((3, D), F32),
        ],
        compiler_params=params(),
        cost_estimate=pl.CostEstimate(
            flops=2 * total * D * (D + FF),
            bytes_accessed=total * (14 * D + 2 * FF) + 2 * D * FF,
            transcendentals=0,
        ),
        name="inner",
    )(*after, pre_low, grad_two, unit_one, inverse_one, w_attn, w_in, rows)


def unattend_kernel(*refs):
    q, k, v, p, ga, stack_out, vec_out = refs[-7:]
    scaling = HEAD ** (-0.5)
    first = pl.program_id(0) == 0

    @pl.when(first)
    def _():
        vec_out[...] = jnp.zeros_like(vec_out)

    for span in range(p.shape[0]):
        at = slice(span * SPAN, (span + 1) * SPAN)
        for pair in range(HEADS // 2):
            lo = pair * 2 * HEAD
            lanes = slice(lo, lo + 2 * HEAD)
            weights = p[span, pair]
            grad = ga[at, lanes]
            spread_out = dot(grad, split_heads(v[at, lanes]), (1, 1))
            wide = weights.astype(F32)
            parts = []
            for half in range(2):
                cols = slice(half * SPAN, (half + 1) * SPAN)
                wgt, gw = wide[:, cols], spread_out[:, cols]
                parts.append((wgt * (gw - jnp.sum(gw * wgt, axis=-1, keepdims=True))).astype(LOW))
            grad_scores = jnp.concatenate(parts, axis=1)
            grad_q = dot(grad_scores, split_heads(k[at, lanes])) * scaling
            tall_scores = jnp.concatenate(parts, axis=0)
            tall_weights = jnp.concatenate([weights[:, :SPAN], weights[:, SPAN:]], axis=0)
            grad_k = dot(tall_scores, split_heads(q[at, lanes]), (0, 0))
            grad_v = dot(tall_weights, split_heads(grad), (0, 0))
            stack_out[at, lo : lo + 2 * HEAD] = grad_q.astype(LOW)
            stack_out[at, D + lo : D + lo + 2 * HEAD] = grad_k.astype(LOW)
            stack_out[at, 2 * D + lo : 2 * D + lo + 2 * HEAD] = grad_v.astype(LOW)
            vec_out[0:1, lanes] += jnp.sum(grad_q, axis=0, keepdims=True)
            vec_out[1:2, lanes] += jnp.sum(grad_v, axis=0, keepdims=True)


def unattend(after, part, parts, q, k, v, p, ga):
    spans = 1
    tall_rows = spans * SPAN
    total = q.shape[0] // parts
    first = part * (total // tall_rows)
    tall = lambda width: pl.BlockSpec((tall_rows, width), lambda i: (first + i, 0))
    return pl.pallas_call(
        unattend_kernel,
        grid=(total // tall_rows,),
        in_specs=[ANY] * len(after)
        + [tall(D)] * 3
        + [
            pl.BlockSpec((spans, HEADS // 2, SPAN, 2 * SPAN), lambda i: (first + i, 0, 0, 0)),
            tall(D),
        ],
        out_specs=[pl.BlockSpec((tall_rows, 3 * D), lambda i: (i, 0)), whole((2, D))],
        out_shape=[
            jax.ShapeDtypeStruct((total, 3 * D), LOW),
            jax.ShapeDtypeStruct((2, D), F32),
        ],
        compiler_params=params(),
        cost_estimate=pl.CostEstimate(
            flops=2 * total * D * 4 * SPAN, bytes_accessed=20 * total * D, transcendentals=0
        ),
        name="unattend",
    )(*after, q, k, v, p, ga)


def input_kernel(*refs):
    grad_one, stack, w_qkv, out = refs[-4:]
    total = grad_one[...]
    for index in range(3):
        total += dot(stack[:, index * D : (index + 1) * D], w_qkv[index], (1, 1))
    out[...] = total


def input_grad(after, grad_one, stack, w_qkv):
    total = grad_one.shape[0]
    tall = lambda width: pl.BlockSpec((TALL, width), lambda i: (i, 0))
    return pl.pallas_call(
        input_kernel,
        grid=(total // TALL,),
        in_specs=[ANY] * len(after) + [tall(D), tall(3 * D), whole(w_qkv.shape)],
        out_specs=tall(D),
        out_shape=jax.ShapeDtypeStruct((total, D), F32),
        compiler_params=params(),
        cost_estimate=pl.CostEstimate(
            flops=6 * total * D * D, bytes_accessed=14 * total * D + 6 * D * D, transcendentals=0
        ),
        name="input",
    )(*after, grad_one, stack, w_qkv)


def contrast_kernel(slots, place, rows, counts, partners, loss_out, grad_out):
    total, scale = rows.shape[0], 2.0 * D ** (-0.5)

    def number(shape, axis):
        at = lax.broadcasted_iota(jnp.int32, shape, axis)
        return (at // GROUP) ^ place[0], at % GROUP

    device, slot = number((counts.shape[1], total), 1)
    hit = lax.broadcasted_iota(jnp.int32, device.shape, 0) == device
    count = dot(counts[...].astype(LOW), jnp.where(hit, 1.0, 0.0).astype(LOW))
    live_across = (slot[:1].astype(F32) < count) & (slot[:1] < slots)
    device, slot = number((total, counts.shape[1]), 0)
    hit = lax.broadcasted_iota(jnp.int32, device.shape, 1) == device
    count = jnp.sum(jnp.where(hit, counts[...], 0.0), axis=1, keepdims=True)
    live_down = (slot[:, :1].astype(F32) < count) & (slot[:, :1] < slots)
    device, slot = number((total, partners.shape[1]), 0)
    own_id = device * slots + slot
    hit = lax.broadcasted_iota(jnp.int32, own_id.shape, 1) == own_id
    pair = jnp.sum(jnp.where(hit, partners[...], 0.0), axis=1, keepdims=True)
    device, slot = number((total, total), 0)
    down = (device * slots + slot).astype(F32)
    device, slot = number((total, total), 1)
    across = (device * slots + slot).astype(F32)
    valid = live_across & (down != across)
    matched = jnp.where((slot < slots) & (pair == across), 1.0, 0.0)
    anchor = jnp.where(live_down & (pair != down[:, :1]), 1.0, 0.0)
    similar = dot(rows[...], rows[...], (1, 1)) * scale
    masked = jnp.where(valid, similar, -1e30)
    peak = jnp.max(masked, axis=1, keepdims=True)
    summed = jnp.sum(jnp.where(valid, jnp.exp(masked - peak), 0.0), axis=1, keepdims=True)
    log_total = jnp.log(summed) + peak
    positive = jnp.sum(matched * similar, axis=1, keepdims=True)
    loss_out[...] = jnp.sum(anchor * (log_total - positive), axis=0, keepdims=True)
    grad = (anchor * (jnp.where(valid, jnp.exp(masked - log_total), 0.0) - matched)).astype(LOW)
    own = lax.broadcasted_iota(jnp.int32, (GROUP, total), 0)
    own = jnp.where(own == lax.broadcasted_iota(jnp.int32, (GROUP, total), 1), 1.0, 0.0)
    down_part = dot(dot(own.astype(LOW), grad, (1, 1)).astype(LOW), rows[...])
    grad_out[...] = (dot(grad[: 2 * GROUP], rows[...])[:GROUP] + down_part) * scale


def contrast(cls_rows, span_count, pair_index, device, slots):
    total = cls_rows.shape[0]
    return pl.pallas_call(
        partial(contrast_kernel, slots),
        in_specs=[pl.BlockSpec(memory_space=pltpu.SMEM)]
        + [pl.BlockSpec(memory_space=pltpu.VMEM)] * 3,
        out_shape=[
            jax.ShapeDtypeStruct((1, 1), F32),
            jax.ShapeDtypeStruct((GROUP, D), F32),
        ],
        compiler_params=params(),
        cost_estimate=pl.CostEstimate(
            flops=2 * total * total * D, bytes_accessed=2 * total * D, transcendentals=2 * total**2
        ),
        name="contrast",
    )(
        device,
        cls_rows,
        span_count.astype(F32).reshape(1, -1),
        pair_index.astype(F32).reshape(1, -1),
    )


def adam_kernel(
    packed, position, gathered, master, first, second, left, right,
    master_out, first_out, second_out, low_out, *scratch,
):
    quarter = D // 4
    slot = pl.program_id(0)
    if packed:
        owned = scratch[0]
        shares, tall, _ = gathered.shape
        rows = D // shares

        @pl.when(slot == 0)
        def _():
            def place(share, carry):
                block = gathered[share].astype(F32)
                at = pl.multiple_of((share ^ position[0]) * rows, rows)
                for index in range(owned.shape[0]):
                    lo = index * rows % tall
                    side = index * rows // tall
                    piece = block[lo : lo + rows, side * quarter : (side + 1) * quarter]
                    owned[index, pl.ds(at, rows), :] = piece
                return carry

            lax.fori_loop(0, shares, place, 0)

        gradient = owned[slot].astype(LOW)
    else:
        gradient = gathered[0]
    low_left, low_right = left[0].astype(LOW), right[0].astype(LOW)
    turned = dot(gradient, low_left, (0, 0))
    turned = dot(low_right, turned.astype(LOW), (0, 0))
    new_first = 0.9 * first[0] + 0.1 * turned
    new_second = 0.999 * second[0] + 0.001 * turned * turned
    first_out[0] = new_first
    second_out[0] = new_second
    spread_by = jnp.sqrt(new_second * (1.0 / (1.0 - 0.999**STEP))) + 1e-08
    update = new_first * (1.0 / (1.0 - 0.9**STEP)) / spread_by
    update = dot(update.astype(LOW), low_left, (1, 1))
    update = dot(low_right, update.astype(LOW))
    new_master = master[0] - RATE * (update + DECAY * master[0])
    master_out[0] = new_master
    low_out[0] = new_master.astype(LOW)


def to_owned(gathered, position, per_owner):
    quarter = D // 4
    gathered = jnp.take(gathered, jnp.arange(gathered.shape[0]) ^ position, axis=0)
    flat = jnp.concatenate([gathered[..., :quarter], gathered[..., quarter:]], axis=1)
    rows = flat.shape[1] // per_owner
    flat = flat.reshape(flat.shape[0], per_owner, rows, quarter).transpose(1, 0, 2, 3)
    return flat.reshape(per_owner, D, quarter)


def rotated_adam(position, gathered, master, first_moment, second_moment, left_basis, right_basis):
    per_owner, _, quarter = master.shape
    turn = lambda a: a.transpose(0, 2, 1)
    rows = D // gathered.shape[0]
    packed = rows % 8 == 0 and per_owner % 2 == 0
    if not packed:
        gathered = to_owned(gathered, position, per_owner)
    block = lambda a: pl.BlockSpec((1,) + a.shape[1:], lambda s, p: (s, 0, 0))
    operands = (turn(master), turn(first_moment), turn(second_moment), left_basis, right_basis)
    like = jax.ShapeDtypeStruct(operands[0].shape, F32)
    fixed = pl.BlockSpec(gathered.shape, lambda s, p: (0, 0, 0))
    outputs = pl.pallas_call(
        partial(adam_kernel, packed),
        grid_spec=pltpu.PrefetchScalarGridSpec(
            num_scalar_prefetch=1,
            grid=(per_owner,),
            in_specs=[fixed if packed else block(gathered)] + [block(a) for a in operands],
            out_specs=[block(operands[0])] * 4,
            scratch_shapes=[pltpu.VMEM((per_owner, D, quarter), F32)] if packed else [],
        ),
        out_shape=[like, like, like, jax.ShapeDtypeStruct(like.shape, LOW)],
        compiler_params=params(),
        cost_estimate=pl.CostEstimate(
            flops=4 * per_owner * D * quarter * (D + quarter),
            bytes_accessed=per_owner * (D * D + 7 * D * quarter) * 4,
            transcendentals=2 * per_owner * D * quarter,
        ),
        name="adam",
    )(position.reshape(1), gathered, *operands)
    return [turn(a) for a in outputs]


def axis_bits(name):
    size = lax.axis_size(name)
    return [(name, 1 << k) for k in range(size.bit_length() - 1)]


def bit_of(step):
    return jnp.where((lax.axis_index(step[0]) & step[1]) != 0, 1, 0)


def swap(send, step):
    size = lax.axis_size(step[0])
    return lax.ppermute(send, step[0], [(i, i ^ step[1]) for i in range(size)])


def pick(array, index, dim):
    return lax.dynamic_index_in_dim(array, index, dim, False)


def gather_all(rows):
    for step in axis_bits("col") + axis_bits("row"):
        rows = jnp.concatenate([rows, swap(rows, step)])
    return rows


def row_steps():
    row_bits, col_bits = axis_bits("row"), axis_bits("col")
    core, across = row_bits[:1], row_bits[1:][::-1]
    y_bits, z_bits = col_bits[:-2][::-1], col_bits[-2:]
    return core, across, y_bits, z_bits


def launch(part, step, left):
    dim = 1 + left.index(step)
    bit = bit_of(step)
    left.remove(step)
    send = pick(part, 1 - bit, dim)
    return send, pick(part, bit, dim), swap(send, step)


def landed(keep, other):
    return (keep.astype(F32) + other.astype(F32)).astype(LOW)


def reduce_panels(send, keep):
    core, across, y_bits, z_bits = row_steps()
    left = across + y_bits + z_bits
    sends = []
    part = landed(keep, swap(send, core[0]))
    width = part.shape[1] >> len(left)
    part = part.reshape(part.shape[:1] + (2,) * len(left) + (width, D))
    sides = [part[..., : D // 2], part[..., D // 2 :]]
    rest = [list(left), list(left)]
    for steps in zip(across + y_bits, y_bits + across):
        moves = [launch(sides[i], steps[i], rest[i]) for i in range(2)]
        sends.append([move[0] for move in moves])
        sides = [landed(move[1], move[2]) for move in moves]
    part, left = jnp.concatenate(sides, axis=-1), list(z_bits)
    for step in z_bits:
        sent, stays, other = launch(part, step, left)
        sends.append([sent])
        part = landed(stays, other)
    return part, sends


def slots_kernel(cols, after, owners, *refs):
    parts, out, shares, packed = refs[after:-3], refs[-3], refs[-2], refs[-1]
    quarter = D // 4
    at = 0
    for part in parts:
        shares[at : at + part.shape[0]] = part[...].astype(F32)
        at += part.shape[0]
    rows, half = shares.shape[1], packed.shape[1]
    slots = at * 4
    for slot in range(slots):
        col, place = divmod(slot, slots // cols)
        owner = owners[slot]
        block = shares[owner // 4]
        which = owner % 4
        value = block[:, :quarter]
        for index in range(1, 4):
            other = block[:, index * quarter : (index + 1) * quarter]
            value = jnp.where(which == index, other, value)
        first = place * rows
        for side in range(2):
            lo, hi = max(first, side * half), min(first + rows, (side + 1) * half)
            if lo < hi:
                lanes = slice(side * quarter, (side + 1) * quarter)
                packed[col, lo - side * half : hi - side * half, lanes] = value[lo - first : hi - first]
    out[...] = packed[...].astype(LOW)


def to_slots(after, parts, owner_list):
    quarter, cols = D // 4, lax.axis_size("col")
    panels, rows = sum(part.shape[0] for part in parts), parts[0].shape[1]
    shape = (cols, panels * 4 // cols * rows // 2, 2 * quarter)
    return pl.pallas_call(
        partial(slots_kernel, cols, len(after)),
        in_specs=[SMEM] + [ANY] * len(after) + [pl.BlockSpec(memory_space=pltpu.VMEM)] * len(parts),
        out_shape=jax.ShapeDtypeStruct(shape, LOW),
        scratch_shapes=[pltpu.VMEM((panels, rows, D), F32), pltpu.VMEM(shape, F32)],
        compiler_params=params(),
        name="slots",
    )(owner_list, *after, *parts)


def spread(slots):
    core, across, y_bits, z_bits = row_steps()
    tail = slots.shape[1:]
    left = axis_bits("col")[::-1]
    part = slots.reshape((1,) + (2,) * len(left) + tail)
    for step in (y_bits + z_bits)[::-1]:
        dim = 1 + left.index(step)
        bit = bit_of(step)
        other = swap(pick(part, 1 - bit, dim), step)
        part = jnp.concatenate([pick(part, bit, dim), other])
        left.remove(step)
    for step in (core + across)[::-1]:
        part = jnp.concatenate([part, swap(part, step)])
    return part


def row_place():
    place = 0
    for group in row_steps():
        for step in group:
            place = place * 2 + bit_of(step)
    return place


def shards(
    tokens,
    w_qkv,
    w_attn_out,
    w_in,
    w_out,
    vectors,
    out_grad,
    span_count,
    pair_index,
    owner_list,
    master,
    first_moment,
    second_moment,
    left_basis,
    right_basis,
    vec_first,
    vec_second,
):
    slots = tokens.shape[0] // SPAN
    device = (lax.axis_index("row") * lax.axis_size("col") + lax.axis_index("col")).reshape(1)
    core, across, y_bits, z_bits = row_steps()
    core_bit = bit_of(core[0])
    rows = vectors.reshape(1, -1)
    q, k, v, p, attended = attend(tokens, w_qkv, rows)
    encoded, hidden, slope, normed_low, unit_one, inverse_one, unit_two, inverse_two = feed(
        device, span_count, tokens, attended, w_attn_out, w_in, w_out, rows
    )
    cls_rows = jnp.pad(encoded.reshape(slots, SPAN, D)[:, 0], ((0, GROUP - slots), (0, 0)))
    loss, grad_cls = contrast(gather_all(cls_rows), span_count, pair_index, device, slots)
    grad_two, outer_low, vec_two = outer_grad(
        device, span_count, out_grad, grad_cls, unit_two, inverse_two, rows
    )
    outer_parts = weight_grad([], core_bit, hidden, outer_low, FF // D, True)
    outer_sum, outer_sent = reduce_panels(*outer_parts)
    pre_low, vec_inner = slope_grad([outer_parts[0]], outer_low, slope, w_out)
    grad_one, mixed_low, grad_attended, vec_one = inner_grad(
        outer_sent[0], pre_low, grad_two, unit_one, inverse_one, w_attn_out, w_in, rows
    )
    inner_parts = weight_grad(
        outer_sent[1], core_bit, normed_low, pre_low, FF // D, False, (attended, mixed_low)
    )
    inner_sum, inner_sent = reduce_panels(*inner_parts)
    early, vec_early = unattend(
        [inner_parts[0]] + outer_sent[2], 0, 2, q, k, v, p, grad_attended
    )
    late, vec_late = unattend(
        [early] + outer_sent[3] + inner_sent[0], 1, 2, q, k, v, p, grad_attended
    )
    stack_low = jnp.concatenate([early, late])
    vec_heads = vec_early + vec_late
    project_parts = weight_grad(
        [outer_sum] + inner_sent[1], core_bit, tokens, stack_low, 3, False
    )
    project_sum, project_sent = reduce_panels(*project_parts)
    grad_tokens = input_grad(
        [project_parts[0]] + inner_sent[2], grad_one, stack_low, w_qkv
    )
    grad_vector = jnp.concatenate(
        [
            jnp.stack([vec_one[0], vec_two[0], vec_one[1], vec_two[1]]),
            vec_heads,
            jnp.stack([vec_one[2], vec_two[2]]),
            vec_inner[:, 0],
        ]
    )
    vec_grad = grad_vector
    for step in core + across + y_bits + z_bits:
        vec_grad += swap(vec_grad, step)
    parts = (project_sum, inner_sum[-1:], inner_sum[:-1], outer_sum)
    gathered = spread(to_slots([grad_tokens, vec_grad], parts, owner_list))
    vec_grad = vec_grad.reshape(-1)
    new_master, new_first, new_second, master_copy = rotated_adam(
        row_place(), gathered, master, first_moment, second_moment, left_basis, right_basis
    )
    vec_first_new = 0.9 * vec_first + 0.1 * vec_grad
    vec_second_new = 0.999 * vec_second + 0.001 * vec_grad * vec_grad
    vec_step = (
        vec_first_new / (1.0 - 0.9**STEP) / (jnp.sqrt(vec_second_new / (1.0 - 0.999**STEP)) + 1e-08)
    )
    vec_new = vectors - VECTOR_RATE * vec_step
    return (
        encoded,
        grad_tokens,
        loss[0, 0],
        new_master,
        new_first,
        new_second,
        master_copy,
        vec_new,
        vec_first_new,
        vec_second_new,
    )


def solution(mesh):
    in_specs = (
        P(("row", "col"), None),
        P(),
        P(),
        P(),
        P(),
        P(),
        P(("row", "col"), None),
        P(),
        P(),
        P(),
        P("col", None, None),
        P("col", None, None),
        P("col", None, None),
        P("col", None, None),
        P("col", None, None),
        P(),
        P(),
    )
    out_specs = (
        P(("row", "col"), None),
        P(("row", "col"), None),
        P(),
        P("col", None, None),
        P("col", None, None),
        P("col", None, None),
        P("col", None, None),
        P(),
        P(),
        P(),
    )
    return jax.shard_map(shards, mesh=mesh, in_specs=in_specs, out_specs=out_specs, check_vma=False)
```

profile of v0, /device:TPU:0, one launch (start us, length us, event | category | flops | bytes accessed | tf_op | source)
XLA Modules:
  0.0 317.2 jit_solution(12924574459402922467)
XLA Ops:
  0.6 10.5 %attend.1 = (bf16[768,768]{1,0:T(8,128)(2,1)}, bf16[768,768]{1,0:T(8,128)(2,1)}, bf16[768,768]{1,0:T(8,128)(2,1)}, bf16[6,6,128,256]{3,2,1,0:T(8,128)(2,1)}, bf16[768,768]{1,0:T(8,128)(2,1)}) custom-call(bf16[768,768]{1,0:T(8,128)(2,1)} %refs_3_.3, bf16[3,768,768]{2,1,0:T(8,128)(2,1)} %refs_4_.1, f32[1,9216]{1,0:T(1,128)} %bitcast.173), custom_call_target="tpu_custom_call" | custom-call | flops 3019898880 | bytes 11796480 | tf_op jit(solution)/shard_map/attend/pallas_call | solution.py:89
  11.1 25.9 %feed.1 = (bf16[768,768]{1,0:T(8,128)(2,1)}, bf16[768,3072]{1,0:T(8,128)(2,1)}, bf16[768,3072]{1,0:T(8,128)(2,1)}, bf16[768,768]{1,0:T(8,128)(2,1)}, bf16[768,76...) custom-call(s32[1]{0:T(128)} %bitcast.place, s32[32]{0:T(128)} %counts.3, ...), custom_call_target="tpu_custom_call" | custom-call | flops 8153726976 | bytes 25952256 | tf_op jit(solution)/shard_map/feed/pallas_call | solution.py:166
  37.9 3.0 collective-permute-start
  46.5 3.0 collective-permute-start.2
  55.5 4.6 %collective-permute-done.4 = bf16[128,768]{1,0:T(8,128)(2,1)S(1)} collective-permute-done((bf16[128,768]{1,0:T(8,128)(2,1)S(1)}, bf16[128,768]{1,0:T(8,128)(2,1)S(1)}, u32[]{:S(2)}, u32[]{:S(2)}) %collective-permute-start.4) | collective-permute-done | bytes 196640 | tf_op jit(solution)/shard_map/ppermute | solution.py:626
  63.6 5.1 %outer.1 = (f32[768,768]{1,0:T(8,128)}, bf16[768,768]{1,0:T(8,128)(2,1)}, f32[3,768]{1,0:T(4,128)}) custom-call(s32[1]{0:T(128)} %bitcast.place, s32[32]{0:T(128)} %counts.3, bf16[768,768]{1,0:T(8,128)(2,1)} %out_grad.1, f32[8,768]{1,0:T(8,128)} %get-tuple-element.51.grad_cls, bf16[768,768]{1,0:T(8,128)(2,1)} %get-tuple-element.52.unit_two, ...), custom_call_target="tpu_custom_call" | custom-call | flops 11796480 | bytes 5898240 | tf_op jit(solution)/shard_map/outer/pallas_call | solution.py:216
  68.7 10.1 %weight.3 = (bf16[4,384,768]{2,1,0:T(8,128)(2,1)}, bf16[4,384,768]{2,1,0:T(8,128)(2,1)}) custom-call(s32[1]{0:T(128)} %bitcast.2.bit, bf16[768,3072]{1,0:T(8,128)(2,1)} %get-tuple-element.50.refs_0_, bf16[768,768]{1,0:T(8,128)(2,1)} %get-tuple-element.54.refs_1_), custom_call_target="tpu_custom_call" | custom-call | flops 3623878656 | bytes 9437184 | tf_op jit(solution)/shard_map/weight/pallas_call | solution.py:279
  78.8 4.7 %collective-permute-done.5 = bf16[4,384,768]{2,1,0:T(8,128)(2,1)S(1)} collective-permute-done((bf16[4,384,768]{2,1,0:T(8,128)(2,1)}, bf16[4,384,768]{2,1,0:T(8,128)(2,1)S(1)}, u32[]{:S(2)}, u32[]{:S(2)}) %collective-permute-start.5) | collective-permute-done | bytes 2359328 | tf_op jit(solution)/shard_map/ppermute | solution.py:626
  88.1 9.1 %slope.1 = (bf16[768,3072]{1,0:T(8,128)(2,1)}, f32[4,1,768]{2,1,0:T(1,128)}) custom-call(bf16[4,384,768]{2,1,0:T(8,128)(2,1)} %get-tuple-element.56.refs_0_, bf16[768,768]{1,0:T(8,128)(2,1)} %get-tuple-element.54.refs_1_, bf16[768,3072]{1,0:T(8,128)(2,1)} %get-tuple-element.58.refs_2_, bf16[3072,768]{1,0:T(8,128)(2,1)} %refs_3_.2), custom_call_target="tpu_custom_call" | custom-call | flops 3623878656 | bytes 14155776 | tf_op jit(solution)/shard_map/slope/pallas_call | solution.py:316
  99.0 12.3 %inner.1 = (f32[768,768]{1,0:T(8,128)}, bf16[768,768]{1,0:T(8,128)(2,1)}, bf16[768,768]{1,0:T(8,128)(2,1)}, f32[3,768]{1,0:T(4,128)}) custom-call(bf16[4,2,2,2,24,384]{5,4,3,2,1,0:T(8,128)(2,1)} %bitcast.165, bf16[4,2,2,2,24,384]{5,4,3,2,1,0:T(8,128)(2,1)} %bitcast.164, bf16[768,3072]{1,0:T(8,128)(2,1)} %get-tuple-element.59.refs_2_.refs_3_, ...), custom_call_target="tpu_custom_call" | custom-call | flops 4529848320 | bytes 17694720 | tf_op jit(solution)/shard_map/inner/pallas_call | solution.py:358
  113.5 13.8 %weight.4 = (bf16[5,384,768]{2,1,0:T(8,128)(2,1)}, bf16[5,384,768]{2,1,0:T(8,128)(2,1)}) custom-call(s32[1]{0:T(128)} %bitcast.2.bit, bf16[4,2,2,24,384]{4,3,2,1,0:T(8,128)(2,1)} %copy.42.refs_0_, bf16[4,2,2,24,384]{4,3,2,1,0:T(8,128)(2,1)} %copy.43.refs_1_, bf16[768,768]{1,0:T(8,128)(2,1)} %get-tuple-element.57.refs_2_, ...), custom_call_target="tpu_custom_call" | custom-call | flops 4529848320 | bytes 11796480 | tf_op jit(solution)/shard_map/weight/pallas_call | solution.py:279
  129.3 7.4 %collective-permute-done.9 = bf16[4,2,2,24,384]{4,3,0,2,1:T(8,128)(2,1)S(1)} collective-permute-done((bf16[4,2,2,24,384]{4,3,0,2,1:T(8,128)(2,1)S(1)}, bf16[4,2,2,24,384]{4,3,0,2,1:T(8,128)(2,1)S(1)}, u32[]{:S(2)}, u32[]{:S(2)}) %collective-permute-start.9) | collective-permute-done | bytes 294944 | tf_op jit(solution)/shard_map/ppermute | solution.py:626
  140.4 8.2 %unattend.2 = (bf16[384,2304]{1,0:T(8,128)(2,1)}, f32[2,768]{1,0:T(2,128)}) custom-call(bf16[5,384,768]{2,1,0:T(8,128)(2,1)} %get-tuple-element.65.refs_0_, bf16[4,2,24,768]{3,2,1,0:T(8,128)(2,1)} %copy.46.refs_1_, bf16[768,768]{1,0:T(8,128)(2,1)} %get-tuple-element.66.refs_2_.refs_4_, bf16[768,768]{1,0:T(8,128)(2,1)} %get-tuple-element.67.refs_3_.refs_5_, ...), custom_call_target="tpu_custom_call" | custom-call | flops 301989888 | bytes 5898240 | tf_op jit(solution)/shard_map/unattend/pallas_call | solution.py:420
  150.4 3.1 collective-permute-start.11
  161.3 8.2 %unattend.3 = (bf16[384,2304]{1,0:T(8,128)(2,1)}, f32[2,768]{1,0:T(2,128)}) custom-call(bf16[384,2304]{1,0:T(8,128)(2,1)} %get-tuple-element.71.refs_0_, bf16[4,24,768]{2,1,0:T(8,128)(2,1)} %copy-done.13, bf16[5,2,2,2,24,384]{5,4,3,2,1,0:T(8,128)(2,1)} %bitcast.160, bf16[5,2,2,2,24,384]{5,4,3,2,1,0:T(8,128)(2,1)} %bitcast.159, ...), custom_call_target="tpu_custom_call" | custom-call | flops 301989888 | bytes 5898240 | tf_op jit(solution)/shard_map/unattend/pallas_call | solution.py:420
  171.1 4.0 %collective-permute-done.14 = bf16[5,2,2,2,24,384]{5,4,0,3,2,1:T(8,128)(2,1)S(1)} collective-permute-done((bf16[5,2,2,2,24,384]{5,4,0,3,2,1:T(8,128)(2,1)S(1)}, bf16[5,2,2,2,24,384]{5,4,0,3,2,1:T(8,128)(2,1)S(1)}, u32[]{:S(2)}, u32[]{:S(2)}) %collective-permute-start.14) | collective-permute-done | bytes 737312 | tf_op jit(solution)/shard_map/ppermute | solution.py:626
  176.2 2.8 collective-permute-done.13
  182.1 9.0 %weight.5 = (bf16[3,384,768]{2,1,0:T(8,128)(2,1)}, bf16[3,384,768]{2,1,0:T(8,128)(2,1)}) custom-call(s32[1]{0:T(128)} %bitcast.2.bit, bf16[4,24,768]{2,1,0:T(8,128)(2,1)} %fusion.24.refs_0_.refs_5_, bf16[5,2,2,24,384]{4,3,2,1,0:T(8,128)(2,1)} %copy.49.refs_1_, bf16[5,2,2,24,384]{4,3,2,1,0:T(8,128)(2,1)} %copy.50.refs_2_, bf16[768,768]{1,0:T(8,128)(2,1)} %refs_3_.3, ...), custom_call_target="tpu_custom_call" | custom-call | flops 2717908992 | bytes 7077888 | tf_op jit(solution)/shard_map/weight/pallas_call | solution.py:279
  196.2 7.3 %collective-permute-done.18 = f32[12,768]{1,0:T(8,128)S(1)} collective-permute-done((f32[12,768]{1,0:T(8,128)S(1)}, f32[12,768]{1,0:T(8,128)S(1)}, u32[]{:S(2)}, u32[]{:S(2)}) %collective-permute-start.18) | collective-permute-done | bytes 36896 | tf_op jit(solution)/shard_map/ppermute | solution.py:626
  204.1 3.6 %collective-permute-done.19 = f32[12,768]{1,0:T(8,128)S(1)} collective-permute-done((f32[12,768]{1,0:T(8,128)S(1)}, f32[12,768]{1,0:T(8,128)S(1)}, u32[]{:S(2)}, u32[]{:S(2)}) %collective-permute-start.19) | collective-permute-done | bytes 36896 | tf_op jit(solution)/shard_map/ppermute | solution.py:626
  207.8 4.1 %collective-permute-done.20 = f32[12,768]{1,0:T(8,128)S(1)} collective-permute-done((f32[12,768]{1,0:T(8,128)S(1)}, f32[12,768]{1,0:T(8,128)S(1)}, u32[]{:S(2)}, u32[]{:S(2)}) %collective-permute-start.20) | collective-permute-done | bytes 36896 | tf_op jit(solution)/shard_map/ppermute | solution.py:626
  212.0 5.0 %collective-permute-done.21 = f32[12,768]{1,0:T(8,128)S(1)} collective-permute-done((f32[12,768]{1,0:T(8,128)S(1)}, f32[12,768]{1,0:T(8,128)S(1)}, u32[]{:S(2)}, u32[]{:S(2)}) %collective-permute-start.21) | collective-permute-done | bytes 36896 | tf_op jit(solution)/shard_map/ppermute | solution.py:626
  223.7 7.8 %input.1.refs_0_ = f32[768,768]{1,0:T(8,128)} custom-call(bf16[3,384,768]{2,1,0:T(8,128)(2,1)} %get-tuple-element.73.refs_0_, bf16[5,2,24,768]{3,2,1,0:T(8,128)(2,1)} %copy.51.refs_1_, f32[768,768]{1,0:T(8,128)} %get-tuple-element.74.refs_2_, bf16[768,2304]{1,0:T(8,128)(2,1)} %copy-done, bf16[3,768,768]{2,1,0:T(8,128)(2,1)} %refs_4_.1), custom_call_target="tpu_custom_call" | custom-call | flops 2717908992 | bytes 11796480 | tf_op jit(solution)/shard_map/input/pallas_call | solution.py:453
  234.5 3.1 collective-permute-done.26
  241.3 6.8 %collective-permute-done.27 = bf16[3,2,24,768]{3,2,0,1:T(8,128)(2,1)S(1)} collective-permute-done((bf16[3,2,24,768]{3,2,0,1:T(8,128)(2,1)S(1)}, bf16[3,2,24,768]{3,2,0,1:T(8,128)(2,1)S(1)}, u32[]{:S(2)}, u32[]{:S(2)}) %collective-permute-start.27) | collective-permute-done | bytes 221216 | tf_op jit(solution)/shard_map/ppermute | solution.py:626
  251.2 3.0 collective-permute-done.28
  254.8 8.5 %slots.1 = bf16[8,72,384]{2,1,0:T(8,128)(2,1)} custom-call(s32[48]{0:T(128)} %owners.1, f32[768,768]{1,0:T(8,128)} %input.1.refs_0_, f32[12,768]{1,0:T(8,128)} %add.208.refs_1_, bf16[3,24,768]{2,1,0:T(8,128)(2,1)} %fusion.37.refs_2_, bf16[1,24,768]{2,1,0:T(8,128)(2,1)} %slice.67.refs_3_, bf16[4,24,768]{2,1,0:T(8,128)(2,1)} %slice.68.refs_4_, ...), custom_call_target="tpu_custom_call" | custom-call | tf_op jit(solution)/shard_map/slots/pallas_call | solution.py:710
  264.5 8.4 %collective-permute-done.31 = bf16[1,2,2,72,384]{4,3,0,2,1:T(8,128)(2,1)S(1)} collective-permute-done((bf16[1,2,2,72,384]{4,3,0,2,1:T(8,128)(2,1)S(1)}, bf16[1,2,2,72,384]{4,3,0,2,1:T(8,128)(2,1)S(1)}, u32[]{:S(2)}, u32[]{:S(2)}) %collective-permute-start.31) | collective-permute-done | bytes 221216 | tf_op jit(solution)/shard_map/ppermute | solution.py:626
  273.0 5.9 %collective-permute-done.32 = bf16[2,2,72,384]{3,2,0,1:T(8,128)(2,1)S(1)} collective-permute-done((bf16[2,2,72,384]{3,2,0,1:T(8,128)(2,1)S(1)}, bf16[2,2,72,384]{3,2,0,1:T(8,128)(2,1)S(1)}, u32[]{:S(2)}, u32[]{:S(2)}) %collective-permute-start.32) | collective-permute-done | bytes 221216 | tf_op jit(solution)/shard_map/ppermute | solution.py:626
  280.6 4.4 %collective-permute-done.33 = bf16[4,72,384]{2,1,0:T(8,128)(2,1)S(1)} collective-permute-done((bf16[4,72,384]{2,1,0:T(8,128)(2,1)S(1)}, bf16[4,72,384]{2,1,0:T(8,128)(2,1)S(1)}, u32[]{:S(2)}, u32[]{:S(2)}) %collective-permute-start.33) | collective-permute-done | bytes 221216 | tf_op jit(solution)/shard_map/ppermute | solution.py:626
  286.5 6.9 %collective-permute-done.34 = bf16[8,72,384]{2,1,0:T(8,128)(2,1)S(1)} collective-permute-done((bf16[8,72,384]{2,1,0:T(8,128)(2,1)S(1)}, bf16[8,72,384]{2,1,0:T(8,128)(2,1)S(1)}, u32[]{:S(2)}, u32[]{:S(2)}) %collective-permute-start.34) | collective-permute-done | bytes 442400 | tf_op jit(solution)/shard_map/ppermute | solution.py:626
  297.5 19.6 %adam.1 = (f32[6,192,768]{2,1,0:T(8,128)}, f32[6,192,768]{2,1,0:T(8,128)}, f32[6,192,768]{2,1,0:T(8,128)}, bf16[6,192,768]{2,1,0:T(8,128)(2,1)}) custom-call(s32[1]{0:T(128)} %bitcast.31.position, bf16[32,72,384]{2,1,0:T(8,128)(2,1)} %pad_maximum_fusion.gathered, f32[6,192,768]{2,1,0:T(8,128)} %bitcast.161, f32[6,192,768]{2,1,0:T(8,128)} %bitcast.162, ...), custom_call_target="tpu_custom_call" | custom-call | flops 3397386240 | bytes 38928384 | tf_op jit(solution)/shard_map/adam/pallas_call | solution.py:594
  (195 shorter events, 76.5 us)
Async XLA Ops:
  37.9 4.7 %collective-permute-start = (bf16[8,768]{1,0:T(8,128)(2,1)S(1)}, bf16[8,768]{1,0:T(8,128)(2,1)S(1)}, u32[]{:S(2)}, u32[]{:S(2)}) collective-permute-start(bf16[8,768]{1,0:T(8,128)(2,1)S(1)} %get-tuple-element.129), channel_id=1, source_target_pairs={{0,1},{1,0},{2,3},{3,2},{4,5},{5,4},{6,7},{7,6},{8,9},{9,8},{10,11... | collective-permute-start | bytes 36872 | tf_op jit(solution)/shard_map/ppermute | solution.py:626
  46.5 5.1 %collective-permute-start.2 = (bf16[32,768]{1,0:T(8,128)(2,1)S(1)}, bf16[32,768]{1,0:T(8,128)(2,1)S(1)}, u32[]{:S(2)}, u32[]{:S(2)}) collective-permute-start(bf16[32,768]{1,0:T(8,128)(2,1)S(1)} %pad_maximum_fusion.4), channel_id=1, source_target_pairs={{0,4},{1,5},{2,6},{3,7},{4,0},{5,1},{6,2},{7,3},{8,12},{9,13},{10,... | collective-permute-start | bytes 147464 | tf_op jit(solution)/shard_map/ppermute | solution.py:626
  53.0 7.1 %collective-permute-start.4 = (bf16[128,768]{1,0:T(8,128)(2,1)S(1)}, bf16[128,768]{1,0:T(8,128)(2,1)S(1)}, u32[]{:S(2)}, u32[]{:S(2)}) collective-permute-start(bf16[128,768]{1,0:T(8,128)(2,1)S(1)} %get-tuple-element.113), channel_id=1, source_target_pairs={{0,16},{8,24},{16,0},{24,8},{1,17},{9,25},{17,1},{25,9},{2,18},{10... | collective-permute-start | bytes 589832 | tf_op jit(solution)/shard_map/ppermute | solution.py:626
  78.8 4.7 %collective-permute-start.5 = (bf16[4,384,768]{2,1,0:T(8,128)(2,1)}, bf16[4,384,768]{2,1,0:T(8,128)(2,1)S(1)}, u32[]{:S(2)}, u32[]{:S(2)}) collective-permute-start(bf16[4,384,768]{2,1,0:T(8,128)(2,1)} %get-tuple-element.56.refs_0_), channel_id=1, source_target_pairs={{0,8},{8,0},{16,24},{24,16},{1,9},{9,1},{17,25},{25,17},{2,10},{10... | collective-permute-start | bytes 7077896 | tf_op jit(solution)/shard_map/ppermute | solution.py:626
  86.3 25.1 %collective-permute-start.8 = (bf16[4,2,2,2,24,384]{5,4,0,3,2,1:T(8,128)(2,1)S(1)}, bf16[4,2,2,2,24,384]{5,4,0,3,2,1:T(8,128)(2,1)S(1)}, u32[]{:S(2)}, u32[]{:S(2)}) collective-permute-start(bf16[4,2,2,2,24,384]{5,4,0,3,2,1:T(8,128)(2,1)S(1)} %bitcast.169), channel_id=1, source_target_pairs={{0,1},{1,0},{2,3},{3,2},{4,5},{5,4},{6,7},{7,6},{8,9},{9,8},{10,11... | collective-permute-start | bytes 1769480 | tf_op jit(solution)/shard_map/ppermute | solution.py:626
  97.4 15.2 %collective-permute-start.6 = (bf16[4,2,2,2,24,384]{5,4,0,3,2,1:T(8,128)(2,1)S(1)}, bf16[4,2,2,2,24,384]{5,4,0,3,2,1:T(8,128)(2,1)S(1)}, u32[]{:S(2)}, u32[]{:S(2)}) collective-permute-start(bf16[4,2,2,2,24,384]{5,4,0,3,2,1:T(8,128)(2,1)S(1)} %bitcast.170), channel_id=1, source_target_pairs={{0,16},{8,24},{16,0},{24,8},{1,17},{9,25},{17,1},{25,9},{2,18},{10... | collective-permute-start | bytes 1769480 | tf_op jit(solution)/shard_map/ppermute | solution.py:626
  127.3 26.2 %collective-permute-start.12 = (bf16[5,384,768]{2,1,0:T(8,128)(2,1)}, bf16[5,384,768]{2,1,0:T(8,128)(2,1)}, u32[]{:S(2)}, u32[]{:S(2)}) collective-permute-start(bf16[5,384,768]{2,1,0:T(8,128)(2,1)} %get-tuple-element.65.refs_0_), channel_id=1, source_target_pairs={{0,8},{8,0},{16,24},{24,16},{1,9},{9,1},{17,25},{25,17},{2,10},{10... | collective-permute-start | bytes 8847368 | tf_op jit(solution)/shard_map/ppermute | solution.py:626
  127.3 9.4 %collective-permute-start.9 = (bf16[4,2,2,24,384]{4,3,0,2,1:T(8,128)(2,1)S(1)}, bf16[4,2,2,24,384]{4,3,0,2,1:T(8,128)(2,1)S(1)}, u32[]{:S(2)}, u32[]{:S(2)}) collective-permute-start(bf16[4,2,2,24,384]{4,3,0,2,1:T(8,128)(2,1)S(1)} %dynamic-slice_bitcast_fusion.2), channel_id=1, source_target_pairs={{0,16},{8,24},{16,0},{24,8},{1,17},{9,25},{17,1},{25,9},{2,18},{10... | collective-permute-start | bytes 884744 | tf_op jit(solution)/shard_map/ppermute | solution.py:626
  128.8 9.1 %collective-permute-start.7 = (bf16[4,2,2,24,384]{4,3,0,2,1:T(8,128)(2,1)S(1)}, bf16[4,2,2,24,384]{4,3,0,2,1:T(8,128)(2,1)S(1)}, u32[]{:S(2)}, u32[]{:S(2)}) collective-permute-start(bf16[4,2,2,24,384]{4,3,0,2,1:T(8,128)(2,1)S(1)} %dynamic-slice_bitcast_fusion.3), channel_id=1, source_target_pairs={{0,1},{1,0},{2,3},{3,2},{4,5},{5,4},{6,7},{7,6},{8,9},{9,8},{10,11... | collective-permute-start | bytes 884744 | tf_op jit(solution)/shard_map/ppermute | solution.py:626
  138.8 11.5 %collective-permute-start.10 = (bf16[4,2,24,768]{3,2,0,1:T(8,128)(2,1)S(1)}, bf16[4,2,24,768]{3,2,0,1:T(8,128)(2,1)S(1)}, u32[]{:S(2)}, u32[]{:S(2)}) collective-permute-start(bf16[4,2,24,768]{3,2,0,1:T(8,128)(2,1)S(1)} %fusion.21), channel_id=1, source_target_pairs={{0,2},{1,3},{2,0},{3,1},{4,6},{5,7},{6,4},{7,5},{8,10},{9,11},{10,... | collective-permute-start | bytes 884744 | tf_op jit(solution)/shard_map/ppermute | solution.py:626
  150.4 9.1 %collective-permute-start.11 = (bf16[4,24,768]{2,1,0:T(8,128)(2,1)S(1)}, bf16[4,24,768]{2,1,0:T(8,128)(2,1)S(1)}, u32[]{:S(2)}, u32[]{:S(2)}) collective-permute-start(bf16[4,24,768]{2,1,0:T(8,128)(2,1)S(1)} %dynamic-slice_bitcast_fusion.9.refs_1_), channel_id=1, source_target_pairs={{0,4},{1,5},{2,6},{3,7},{4,0},{5,1},{6,2},{7,3},{8,12},{9,13},{10,... | collective-permute-start | bytes 442376 | tf_op jit(solution)/shard_map/ppermute | solution.py:626
  157.8 17.3 %collective-permute-start.14 = (bf16[5,2,2,2,24,384]{5,4,0,3,2,1:T(8,128)(2,1)S(1)}, bf16[5,2,2,2,24,384]{5,4,0,3,2,1:T(8,128)(2,1)S(1)}, u32[]{:S(2)}, u32[]{:S(2)}) collective-permute-start(bf16[5,2,2,2,24,384]{5,4,0,3,2,1:T(8,128)(2,1)S(1)} %bitcast.167), channel_id=1, source_target_pairs={{0,1},{1,0},{2,3},{3,2},{4,5},{5,4},{6,7},{7,6},{8,9},{9,8},{10,11... | collective-permute-start | bytes 2211848 | tf_op jit(solution)/shard_map/ppermute | solution.py:626
  160.5 18.5 %collective-permute-start.13 = (bf16[5,2,2,2,24,384]{5,4,0,3,2,1:T(8,128)(2,1)S(1)}, bf16[5,2,2,2,24,384]{5,4,0,3,2,1:T(8,128)(2,1)S(1)}, u32[]{:S(2)}, u32[]{:S(2)}) collective-permute-start(bf16[5,2,2,2,24,384]{5,4,0,3,2,1:T(8,128)(2,1)S(1)} %bitcast.168), channel_id=1, source_target_pairs={{0,16},{8,24},{16,0},{24,8},{1,17},{9,25},{17,1},{25,9},{2,18},{10... | collective-permute-start | bytes 2211848 | tf_op jit(solution)/shard_map/ppermute | solution.py:626
  191.1 27.6 %collective-permute-start.22 = (bf16[3,384,768]{2,1,0:T(8,128)(2,1)}, bf16[3,384,768]{2,1,0:T(8,128)(2,1)}, u32[]{:S(2)}, u32[]{:S(2)}) collective-permute-start(bf16[3,384,768]{2,1,0:T(8,128)(2,1)} %get-tuple-element.73.refs_0_), channel_id=1, source_target_pairs={{0,8},{8,0},{16,24},{24,16},{1,9},{9,1},{17,25},{25,17},{2,10},{10... | collective-permute-start | bytes 5308424 | tf_op jit(solution)/shard_map/ppermute | solution.py:626
  191.3 26.3 %collective-permute-start.16 = (bf16[5,2,2,24,384]{4,3,0,2,1:T(8,128)(2,1)}, bf16[5,2,2,24,384]{4,3,0,2,1:T(8,128)(2,1)}, u32[]{:S(2)}, u32[]{:S(2)}) collective-permute-start(bf16[5,2,2,24,384]{4,3,0,2,1:T(8,128)(2,1)} %dynamic-slice_bitcast_fusion), channel_id=1, source_target_pairs={{0,16},{8,24},{16,0},{24,8},{1,17},{9,25},{17,1},{25,9},{2,18},{10... | collective-permute-start | bytes 1105928 | tf_op jit(solution)/shard_map/ppermute | solution.py:626
  195.0 8.6 %collective-permute-start.18 = (f32[12,768]{1,0:T(8,128)S(1)}, f32[12,768]{1,0:T(8,128)S(1)}, u32[]{:S(2)}, u32[]{:S(2)}) collective-permute-start(f32[12,768]{1,0:T(8,128)S(1)} %add.204), channel_id=1, source_target_pairs={{0,16},{8,24},{16,0},{24,8},{1,17},{9,25},{17,1},{25,9},{2,18},{10... | collective-permute-start | bytes 110600 | tf_op jit(solution)/shard_map/ppermute | solution.py:626
  195.7 22.9 %collective-permute-start.15 = (bf16[5,2,2,24,384]{4,3,0,2,1:T(8,128)(2,1)}, bf16[5,2,2,24,384]{4,3,0,2,1:T(8,128)(2,1)S(1)}, u32[]{:S(2)}, u32[]{:S(2)}) collective-permute-start(bf16[5,2,2,24,384]{4,3,0,2,1:T(8,128)(2,1)} %copy-done.12), channel_id=1, source_target_pairs={{0,1},{1,0},{2,3},{3,2},{4,5},{5,4},{6,7},{7,6},{8,9},{9,8},{10,11... | collective-permute-start | bytes 1105928 | tf_op jit(solution)/shard_map/ppermute | solution.py:626
  203.6 4.2 %collective-permute-start.19 = (f32[12,768]{1,0:T(8,128)S(1)}, f32[12,768]{1,0:T(8,128)S(1)}, u32[]{:S(2)}, u32[]{:S(2)}) collective-permute-start(f32[12,768]{1,0:T(8,128)S(1)} %add.205), channel_id=1, source_target_pairs={{0,1},{1,0},{2,3},{3,2},{4,5},{5,4},{6,7},{7,6},{8,9},{9,8},{10,11... | collective-permute-start | bytes 110600 | tf_op jit(solution)/shard_map/ppermute | solution.py:626
  207.7 4.2 %collective-permute-start.20 = (f32[12,768]{1,0:T(8,128)S(1)}, f32[12,768]{1,0:T(8,128)S(1)}, u32[]{:S(2)}, u32[]{:S(2)}) collective-permute-start(f32[12,768]{1,0:T(8,128)S(1)} %add.206), channel_id=1, source_target_pairs={{0,2},{1,3},{2,0},{3,1},{4,6},{5,7},{6,4},{7,5},{8,10},{9,11},{10,... | collective-permute-start | bytes 110600 | tf_op jit(solution)/shard_map/ppermute | solution.py:626
  211.9 5.0 %collective-permute-start.21 = (f32[12,768]{1,0:T(8,128)S(1)}, f32[12,768]{1,0:T(8,128)S(1)}, u32[]{:S(2)}, u32[]{:S(2)}) collective-permute-start(f32[12,768]{1,0:T(8,128)S(1)} %add.207), channel_id=1, source_target_pairs={{0,4},{1,5},{2,6},{3,7},{4,0},{5,1},{6,2},{7,3},{8,12},{9,13},{10,... | collective-permute-start | bytes 110600 | tf_op jit(solution)/shard_map/ppermute | solution.py:626
  221.1 10.3 %collective-permute-start.25 = (bf16[3,2,2,2,24,384]{5,4,0,3,2,1:T(8,128)(2,1)S(1)}, bf16[3,2,2,2,24,384]{5,4,0,3,2,1:T(8,128)(2,1)S(1)}, u32[]{:S(2)}, u32[]{:S(2)}) collective-permute-start(bf16[3,2,2,2,24,384]{5,4,0,3,2,1:T(8,128)(2,1)S(1)} %bitcast.171), channel_id=1, source_target_pairs={{0,1},{1,0},{2,3},{3,2},{4,5},{5,4},{6,7},{7,6},{8,9},{9,8},{10,11... | collective-permute-start | bytes 1327112 | tf_op jit(solution)/shard_map/ppermute | solution.py:626
  221.7 19.4 %collective-permute-start.29 = (bf16[5,2,24,768]{3,2,0,1:T(8,128)(2,1)S(1)}, bf16[5,2,24,768]{3,2,0,1:T(8,128)(2,1)S(1)}, u32[]{:S(2)}, u32[]{:S(2)}) collective-permute-start(bf16[5,2,24,768]{3,2,0,1:T(8,128)(2,1)S(1)} %fusion.18), channel_id=1, source_target_pairs={{0,2},{1,3},{2,0},{3,1},{4,6},{5,7},{6,4},{7,5},{8,10},{9,11},{10,... | collective-permute-start | bytes 1105928 | tf_op jit(solution)/shard_map/ppermute | solution.py:626
  222.7 10.1 %collective-permute-start.23 = (bf16[3,2,2,2,24,384]{5,4,0,3,2,1:T(8,128)(2,1)S(1)}, bf16[3,2,2,2,24,384]{5,4,0,3,2,1:T(8,128)(2,1)S(1)}, u32[]{:S(2)}, u32[]{:S(2)}) collective-permute-start(bf16[3,2,2,2,24,384]{5,4,0,3,2,1:T(8,128)(2,1)S(1)} %bitcast.172), channel_id=1, source_target_pairs={{0,16},{8,24},{16,0},{24,8},{1,17},{9,25},{17,1},{25,9},{2,18},{10... | collective-permute-start | bytes 1327112 | tf_op jit(solution)/shard_map/ppermute | solution.py:626
  231.6 6.0 %collective-permute-start.26 = (bf16[3,2,2,24,384]{4,3,0,2,1:T(8,128)(2,1)S(1)}, bf16[3,2,2,24,384]{4,3,0,2,1:T(8,128)(2,1)S(1)}, u32[]{:S(2)}, u32[]{:S(2)}) collective-permute-start(bf16[3,2,2,24,384]{4,3,0,2,1:T(8,128)(2,1)S(1)} %dynamic-slice_bitcast_fusion.6), channel_id=1, source_target_pairs={{0,16},{8,24},{16,0},{24,8},{1,17},{9,25},{17,1},{25,9},{2,18},{10... | collective-permute-start | bytes 663560 | tf_op jit(solution)/shard_map/ppermute | solution.py:626
  232.9 6.0 %collective-permute-start.24 = (bf16[3,2,2,24,384]{4,3,0,2,1:T(8,128)(2,1)S(1)}, bf16[3,2,2,24,384]{4,3,0,2,1:T(8,128)(2,1)S(1)}, u32[]{:S(2)}, u32[]{:S(2)}) collective-permute-start(bf16[3,2,2,24,384]{4,3,0,2,1:T(8,128)(2,1)S(1)} %dynamic-slice_bitcast_fusion.7), channel_id=1, source_target_pairs={{0,1},{1,0},{2,3},{3,2},{4,5},{5,4},{6,7},{7,6},{8,9},{9,8},{10,11... | collective-permute-start | bytes 663560 | tf_op jit(solution)/shard_map/ppermute | solution.py:626
  239.0 9.1 %collective-permute-start.27 = (bf16[3,2,24,768]{3,2,0,1:T(8,128)(2,1)S(1)}, bf16[3,2,24,768]{3,2,0,1:T(8,128)(2,1)S(1)}, u32[]{:S(2)}, u32[]{:S(2)}) collective-permute-start(bf16[3,2,24,768]{3,2,0,1:T(8,128)(2,1)S(1)} %fusion.34), channel_id=1, source_target_pairs={{0,2},{1,3},{2,0},{3,1},{4,6},{5,7},{6,4},{7,5},{8,10},{9,11},{10,... | collective-permute-start | bytes 663560 | tf_op jit(solution)/shard_map/ppermute | solution.py:626
  241.2 8.6 %collective-permute-start.30 = (bf16[5,24,768]{2,1,0:T(8,128)(2,1)S(1)}, bf16[5,24,768]{2,1,0:T(8,128)(2,1)S(1)}, u32[]{:S(2)}, u32[]{:S(2)}) collective-permute-start(bf16[5,24,768]{2,1,0:T(8,128)(2,1)S(1)} %dynamic-slice_bitcast_fusion.8), channel_id=1, source_target_pairs={{0,4},{1,5},{2,6},{3,7},{4,0},{5,1},{6,2},{7,3},{8,12},{9,13},{10,... | collective-permute-start | bytes 552968 | tf_op jit(solution)/shard_map/ppermute | solution.py:626
  248.3 5.9 %collective-permute-start.28 = (bf16[3,24,768]{2,1,0:T(8,128)(2,1)S(1)}, bf16[3,24,768]{2,1,0:T(8,128)(2,1)S(1)}, u32[]{:S(2)}, u32[]{:S(2)}) collective-permute-start(bf16[3,24,768]{2,1,0:T(8,128)(2,1)S(1)} %dynamic-slice_bitcast_fusion.10), channel_id=1, source_target_pairs={{0,4},{1,5},{2,6},{3,7},{4,0},{5,1},{6,2},{7,3},{8,12},{9,13},{10,... | collective-permute-start | bytes 331784 | tf_op jit(solution)/shard_map/ppermute | solution.py:626
  264.4 8.4 %collective-permute-start.31 = (bf16[1,2,2,72,384]{4,3,0,2,1:T(8,128)(2,1)S(1)}, bf16[1,2,2,72,384]{4,3,0,2,1:T(8,128)(2,1)S(1)}, u32[]{:S(2)}, u32[]{:S(2)}) collective-permute-start(bf16[1,2,2,72,384]{4,3,0,2,1:T(8,128)(2,1)S(1)} %get-tuple-element.111), channel_id=1, source_target_pairs={{0,4},{1,5},{2,6},{3,7},{4,0},{5,1},{6,2},{7,3},{8,12},{9,13},{10,... | collective-permute-start | bytes 663560 | tf_op jit(solution)/shard_map/ppermute | solution.py:626
  272.9 6.0 %collective-permute-start.32 = (bf16[2,2,72,384]{3,2,0,1:T(8,128)(2,1)S(1)}, bf16[2,2,72,384]{3,2,0,1:T(8,128)(2,1)S(1)}, u32[]{:S(2)}, u32[]{:S(2)}) collective-permute-start(bf16[2,2,72,384]{3,2,0,1:T(8,128)(2,1)S(1)} %get-tuple-element.109), channel_id=1, source_target_pairs={{0,2},{1,3},{2,0},{3,1},{4,6},{5,7},{6,4},{7,5},{8,10},{9,11},{10,... | collective-permute-start | bytes 663560 | tf_op jit(solution)/shard_map/ppermute | solution.py:626
  279.0 6.0 %collective-permute-start.33 = (bf16[4,72,384]{2,1,0:T(8,128)(2,1)S(1)}, bf16[4,72,384]{2,1,0:T(8,128)(2,1)S(1)}, u32[]{:S(2)}, u32[]{:S(2)}) collective-permute-start(bf16[4,72,384]{2,1,0:T(8,128)(2,1)S(1)} %get-tuple-element.108), channel_id=1, source_target_pairs={{0,1},{1,0},{2,3},{3,2},{4,5},{5,4},{6,7},{7,6},{8,9},{9,8},{10,11... | collective-permute-start | bytes 663560 | tf_op jit(solution)/shard_map/ppermute | solution.py:626
  285.1 8.4 %collective-permute-start.34 = (bf16[8,72,384]{2,1,0:T(8,128)(2,1)S(1)}, bf16[8,72,384]{2,1,0:T(8,128)(2,1)S(1)}, u32[]{:S(2)}, u32[]{:S(2)}) collective-permute-start(bf16[8,72,384]{2,1,0:T(8,128)(2,1)S(1)} %pad_maximum_fusion.2), channel_id=1, source_target_pairs={{0,16},{8,24},{16,0},{24,8},{1,17},{9,25},{17,1},{25,9},{2,18},{10... | collective-permute-start | bytes 1327112 | tf_op jit(solution)/shard_map/ppermute | solution.py:626
  (30 other events, 331.6 us)
where the time goes:
time: 318 us; the launch traced here: 317 us
  Pallas kernels  151 us (47%)
  waiting for transfers between devices  97.9 us (31%)
  starting transfers between devices  34.4 us (11%)
  local copies, waits for them, and re-layouts  17.6 us (6%)
  other arithmetic  15.1 us (5%)
    ppermute x36, waiting for transfers between devices, swap(): return lax.ppermute(send, step[0], [(i, i ^ step[1]) for i in range(size)])  97.9 us
    ppermute x36, starting transfers between devices, swap(): return lax.ppermute(send, step[0], [(i, i ^ step[1]) for i in range(size)])  34.4 us
    pallas_call x3, Pallas kernels, weight_grad(): pl.pallas_call(partial(weight_kernel, panels, len(after)), grid_spec=pltp...  32.9 us
    pallas_call x1, Pallas kernels, feed(): pl.pallas_call(feed_kernel, grid=(total // TALL,), in_specs=[SMEM, SMEM,...  25.9 us
    pallas_call x1, Pallas kernels, rotated_adam(): pl.pallas_call(partial(adam_kernel, packed), grid_spec=pltpu.PrefetchScal...  19.6 us
    pallas_call x2, Pallas kernels, unattend(): pl.pallas_call(unattend_kernel, grid=(total // tall_rows,), in_specs=[ANY...  16.3 us
    pallas_call x1, Pallas kernels, inner_grad(): pl.pallas_call(inner_kernel, grid=(total // TALL,), in_specs=[ANY] * len(...  12.3 us
    convert_element_type x21, other arithmetic, landed(): return (keep.astype(F32) + other.astype(F32)).astype(LOW)  10.8 us
  transfers between devices with their start and end apart: 36, of which 27 were waited for; matrix products, arithmetic and copies ran while one was open for 6% of the time, Pallas kernels for 14%

commit v1 on v0

--- a/solution.py
+++ b/solution.py
@@ -32,6 +32,12 @@
 
 def whole(shape):
     return pl.BlockSpec(shape, lambda *ids: (0,) * len(shape))
+
+
+def cost(microseconds, transcendentals=0):
+    return pl.CostEstimate(
+        flops=int(microseconds * 1.1e9), bytes_accessed=0, transcendentals=transcendentals
+    )
 
 
 def params():
@@ -105,11 +111,7 @@
             like,
         ],
         compiler_params=params(),
-        cost_estimate=pl.CostEstimate(
-            flops=2 * total * D * (3 * D + 2 * SPAN),
-            bytes_accessed=14 * total * D + 6 * D * D,
-            transcendentals=total * HEADS * SPAN,
-        ),
+        cost_estimate=cost(10),
         name="attend",
     )(tokens, w_qkv, rows)
 
@@ -174,11 +176,7 @@
             like(D, LOW), like(1, F32), like(D, LOW), like(1, F32),
         ],
         compiler_params=params(),
-        cost_estimate=pl.CostEstimate(
-            flops=2 * total * D * (D + 2 * FF),
-            bytes_accessed=total * (12 * D + 4 * FF) + 4 * D * FF,
-            transcendentals=total * FF * 2,
-        ),
+        cost_estimate=cost(26),
         name="feed",
     )(place, counts, tokens, attended, w_attn, w_in, w_out, rows)
 
@@ -222,82 +220,49 @@
             jax.ShapeDtypeStruct((3, D), F32),
         ],
         compiler_params=params(),
-        cost_estimate=pl.CostEstimate(
-            flops=20 * total * D, bytes_accessed=10 * total * D, transcendentals=0
-        ),
+        cost_estimate=cost(5),
         name="outer",
     )(place, counts, out_grad, grad_cls, unit_two, inverse_two, rows)
 
 
-def weight_kernel(panels, ordered_after, bit, *refs):
-    left_side, right_side, *rest = refs[ordered_after:]
-    extra_left, extra_right = rest[:-2] or (None, None)
-    send_out, keep_out = rest[-2:]
-
-    def store(left_from, right_from):
-        value = dot(left_from[...], right_from[...], (0, 0)).astype(LOW)
-
-        @pl.when(pl.program_id(0) == 0)
+def weight_kernel(panels, after, side, *refs):
+    *sides, out = refs[after:]
+
+    @pl.when(pl.program_id(0) < panels)
+    def _():
+        out[0] = dot(sides[0][...], sides[1][...], (0, 0)).astype(LOW)
+
+    if len(sides) > 2:
+
+        @pl.when(pl.program_id(0) == panels)
         def _():
-            send_out[0] = value
-
-        @pl.when(pl.program_id(0) == 1)
-        def _():
-            keep_out[0] = value
-
-    if extra_left is None:
-        store(left_side, right_side)
-        return
-
-    @pl.when(pl.program_id(1) < panels)
-    def _():
-        store(left_side, right_side)
-
-    @pl.when(pl.program_id(1) == panels)
-    def _():
-        store(extra_left, extra_right)
-
-
-def weight_grad(after, bit, left_side, right_side, panels, banded, extra=()):
+            out[0] = dot(sides[2][...], sides[3][...], (0, 0)).astype(LOW)
+
+
+def weight_half(hint, after, side, left_side, right_side, panels, banded, extra=()):
     total = left_side.shape[0]
     half = D // 2
     every = panels + len(extra) // 2
-
-    def side_of(phase, bit):
-        return jnp.where(phase == 0, 1 - bit[0], bit[0])
-
-    def left_at(phase, panel, bit):
-        side = side_of(phase, bit)
-        return (0, jnp.minimum(panel, panels - 1) * 2 + side if banded else side)
-
-    def right_at(phase, panel, bit):
-        return (0, 0 if banded else jnp.minimum(panel, panels - 1))
-
-    like = jax.ShapeDtypeStruct((every, half, D), LOW)
     tall = lambda width, at: pl.BlockSpec((total, width), at)
-    more = [tall(half, lambda f, p, b: (0, side_of(f, b))), tall(D, lambda f, p, b: (0, 0))]
+    last = lambda panel: jnp.minimum(panel, panels - 1)
+    left_at = lambda panel, side: (0, last(panel) * 2 + side[0] if banded else side[0])
+    right_at = lambda panel, side: (0, 0 if banded else last(panel))
+    more = [tall(half, lambda p, s: (0, s[0])), tall(D, lambda p, s: (0, 0))]
     return pl.pallas_call(
         partial(weight_kernel, panels, len(after)),
         grid_spec=pltpu.PrefetchScalarGridSpec(
             num_scalar_prefetch=1,
-            grid=(2, every),
+            grid=(every,),
             in_specs=[ANY] * len(after)
             + [tall(half, left_at), tall(D, right_at)]
             + more[: len(extra)],
-            out_specs=[
-                pl.BlockSpec((1, half, D), lambda f, p, b: (jnp.where(f == 0, p, every - 1), 0, 0)),
-                pl.BlockSpec((1, half, D), lambda f, p, b: (jnp.where(f == 0, 0, p), 0, 0)),
-            ],
+            out_specs=pl.BlockSpec((1, half, D), lambda p, s: (p, 0, 0)),
         ),
-        out_shape=[like, like],
-        compiler_params=params(),
-        cost_estimate=pl.CostEstimate(
-            flops=2 * total * D * D * every,
-            bytes_accessed=2 * (total + D) * D * every,
-            transcendentals=0,
-        ),
+        out_shape=jax.ShapeDtypeStruct((every, half, D), LOW),
+        compiler_params=params(),
+        cost_estimate=cost(hint),
         name="weight",
-    )(bit.reshape(1), *after, left_side, right_side, *extra)
+    )(side.reshape(1), *after, left_side, right_side, *extra)
 
 
 def slope_kernel(*refs):
@@ -324,9 +289,7 @@
             jax.ShapeDtypeStruct((FF // D, 1, D), F32),
         ],
         compiler_params=params(),
-        cost_estimate=pl.CostEstimate(
-            flops=2 * total * D * FF, bytes_accessed=4 * total * FF + 2 * D * FF, transcendentals=0
-        ),
+        cost_estimate=cost(9),
         name="slope",
     )(*after, low, slope, w_out)
 
@@ -366,11 +329,7 @@
             like(D, F32), like(D, LOW), like(D, LOW), jax.ShapeDtypeStruct((3, D), F32),
         ],
         compiler_params=params(),
-        cost_estimate=pl.CostEstimate(
-            flops=2 * total * D * (D + FF),
-            bytes_accessed=total * (14 * D + 2 * FF) + 2 * D * FF,
-            transcendentals=0,
-        ),
+        cost_estimate=cost(12),
         name="inner",
     )(*after, pre_low, grad_two, unit_one, inverse_one, w_attn, w_in, rows)
 
@@ -411,30 +370,29 @@
             vec_out[1:2, lanes] += jnp.sum(grad_v, axis=0, keepdims=True)
 
 
-def unattend(after, part, parts, q, k, v, p, ga):
-    spans = 1
-    tall_rows = spans * SPAN
-    total = q.shape[0] // parts
-    first = part * (total // tall_rows)
-    tall = lambda width: pl.BlockSpec((tall_rows, width), lambda i: (first + i, 0))
+def unattend(after, part, parts, q, k, v, p, ga, stack=None):
+    total = q.shape[0]
+    count = total // SPAN // parts
+    first = part * count
+    tall = lambda width: pl.BlockSpec((SPAN, width), lambda i: (first + i, 0))
+    after = after if stack is None else [stack] + after
     return pl.pallas_call(
         unattend_kernel,
-        grid=(total // tall_rows,),
+        grid=(count,),
         in_specs=[ANY] * len(after)
         + [tall(D)] * 3
         + [
-            pl.BlockSpec((spans, HEADS // 2, SPAN, 2 * SPAN), lambda i: (first + i, 0, 0, 0)),
+            pl.BlockSpec((1, HEADS // 2, SPAN, 2 * SPAN), lambda i: (first + i, 0, 0, 0)),
             tall(D),
         ],
-        out_specs=[pl.BlockSpec((tall_rows, 3 * D), lambda i: (i, 0)), whole((2, D))],
+        out_specs=[tall(3 * D), whole((2, D))],
         out_shape=[
             jax.ShapeDtypeStruct((total, 3 * D), LOW),
             jax.ShapeDtypeStruct((2, D), F32),
         ],
-        compiler_params=params(),
-        cost_estimate=pl.CostEstimate(
-            flops=2 * total * D * 4 * SPAN, bytes_accessed=20 * total * D, transcendentals=0
-        ),
+        input_output_aliases={} if stack is None else {0: 0},
+        compiler_params=params(),
+        cost_estimate=cost(8),
         name="unattend",
     )(*after, q, k, v, p, ga)
 
@@ -457,9 +415,7 @@
         out_specs=tall(D),
         out_shape=jax.ShapeDtypeStruct((total, D), F32),
         compiler_params=params(),
-        cost_estimate=pl.CostEstimate(
-            flops=6 * total * D * D, bytes_accessed=14 * total * D + 6 * D * D, transcendentals=0
-        ),
+        cost_estimate=cost(8),
         name="input",
     )(*after, grad_one, stack, w_qkv)
 
@@ -515,9 +471,7 @@
             jax.ShapeDtypeStruct((GROUP, D), F32),
         ],
         compiler_params=params(),
-        cost_estimate=pl.CostEstimate(
-            flops=2 * total * total * D, bytes_accessed=2 * total * D, transcendentals=2 * total**2
-        ),
+        cost_estimate=cost(3),
         name="contrast",
     )(
         device,
@@ -602,11 +556,7 @@
         ),
         out_shape=[like, like, like, jax.ShapeDtypeStruct(like.shape, LOW)],
         compiler_params=params(),
-        cost_estimate=pl.CostEstimate(
-            flops=4 * per_owner * D * quarter * (D + quarter),
-            bytes_accessed=per_owner * (D * D + 7 * D * quarter) * 4,
-            transcendentals=2 * per_owner * D * quarter,
-        ),
+        cost_estimate=cost(20),
         name="adam",
     )(position.reshape(1), gathered, *operands)
     return [turn(a) for a in outputs]
@@ -643,57 +593,67 @@
     return core, across, y_bits, z_bits
 
 
-def launch(part, step, left):
+def launch(part, step, left, rider=None):
     dim = 1 + left.index(step)
     bit = bit_of(step)
     left.remove(step)
-    send = pick(part, 1 - bit, dim)
-    return send, pick(part, bit, dim), swap(send, step)
+    send, keep = pick(part, 1 - bit, dim), pick(part, bit, dim)
+    shape, flat = send.shape, send.reshape(-1, send.shape[-1])
+    message = flat
+    if rider is not None:
+        message = jnp.concatenate([flat, rider.astype(LOW).reshape(-1, flat.shape[1])])
+    other = swap(message, step)
+    total = landed(keep, other[: flat.shape[0]].reshape(shape))
+    if rider is not None:
+        rider = rider + other[flat.shape[0] :].reshape(rider.shape).astype(F32)
+    return message, total, rider
 
 
 def landed(keep, other):
     return (keep.astype(F32) + other.astype(F32)).astype(LOW)
 
 
-def reduce_panels(send, keep):
+def begin_sum(send):
+    return swap(send, row_steps()[0][0])
+
+
+def reduce_panels(other, keep, rider=None):
     core, across, y_bits, z_bits = row_steps()
     left = across + y_bits + z_bits
     sends = []
-    part = landed(keep, swap(send, core[0]))
+    part = landed(keep, other)
+    if rider is not None:
+        rider = rider + swap(rider, core[0])
     width = part.shape[1] >> len(left)
     part = part.reshape(part.shape[:1] + (2,) * len(left) + (width, D))
     sides = [part[..., : D // 2], part[..., D // 2 :]]
     rest = [list(left), list(left)]
-    for steps in zip(across + y_bits, y_bits + across):
-        moves = [launch(sides[i], steps[i], rest[i]) for i in range(2)]
-        sends.append([move[0] for move in moves])
-        sides = [landed(move[1], move[2]) for move in moves]
+    for first, second in zip(across + y_bits, y_bits + across):
+        sent, one, rider = launch(sides[0], first, rest[0], rider)
+        also, two, _ = launch(sides[1], second, rest[1])
+        sends.append([sent, also])
+        sides = [one, two]
     part, left = jnp.concatenate(sides, axis=-1), list(z_bits)
     for step in z_bits:
-        sent, stays, other = launch(part, step, left)
+        sent, part, rider = launch(part, step, left, rider)
         sends.append([sent])
-        part = landed(stays, other)
-    return part, sends
+    return part, sends, rider
 
 
 def slots_kernel(cols, after, owners, *refs):
-    parts, out, shares, packed = refs[after:-3], refs[-3], refs[-2], refs[-1]
+    parts, out, blocks, packed = refs[after:-3], refs[-3], refs[-2], refs[-1]
     quarter = D // 4
     at = 0
     for part in parts:
-        shares[at : at + part.shape[0]] = part[...].astype(F32)
-        at += part.shape[0]
-    rows, half = shares.shape[1], packed.shape[1]
-    slots = at * 4
-    for slot in range(slots):
-        col, place = divmod(slot, slots // cols)
-        owner = owners[slot]
-        block = shares[owner // 4]
-        which = owner % 4
-        value = block[:, :quarter]
-        for index in range(1, 4):
-            other = block[:, index * quarter : (index + 1) * quarter]
-            value = jnp.where(which == index, other, value)
+        for panel in range(part.shape[0]):
+            value = part[panel].astype(F32)
+            for index in range(4):
+                blocks[at] = value[:, index * quarter : (index + 1) * quarter]
+                at += 1
+    rows, half = blocks.shape[1], packed.shape[1]
+    for slot in range(at):
+        col, place = divmod(slot, at // cols)
+        value = blocks[owners[slot]]
         first = place * rows
         for side in range(2):
             lo, hi = max(first, side * half), min(first + rows, (side + 1) * half)
@@ -711,8 +671,9 @@
         partial(slots_kernel, cols, len(after)),
         in_specs=[SMEM] + [ANY] * len(after) + [pl.BlockSpec(memory_space=pltpu.VMEM)] * len(parts),
         out_shape=jax.ShapeDtypeStruct(shape, LOW),
-        scratch_shapes=[pltpu.VMEM((panels, rows, D), F32), pltpu.VMEM(shape, F32)],
-        compiler_params=params(),
+        scratch_shapes=[pltpu.VMEM((panels * 4, rows, quarter), F32), pltpu.VMEM(shape, F32)],
+        compiler_params=params(),
+        cost_estimate=cost(4),
         name="slots",
     )(owner_list, *after, *parts)
 
@@ -774,31 +735,26 @@
     grad_two, outer_low, vec_two = outer_grad(
         device, span_count, out_grad, grad_cls, unit_two, inverse_two, rows
     )
-    outer_parts = weight_grad([], core_bit, hidden, outer_low, FF // D, True)
-    outer_sum, outer_sent = reduce_panels(*outer_parts)
-    pre_low, vec_inner = slope_grad([outer_parts[0]], outer_low, slope, w_out)
+    outer_args = (hidden, outer_low, FF // D, True)
+    outer_away = weight_half(8, [], 1 - core_bit, *outer_args)
+    outer_here = weight_half(60, [outer_away], core_bit, *outer_args)
+    outer_sum, outer_sent, _ = reduce_panels(begin_sum(outer_away), outer_here)
+    pre_low, vec_inner = slope_grad(outer_sent[0], outer_low, slope, w_out)
     grad_one, mixed_low, grad_attended, vec_one = inner_grad(
-        outer_sent[0], pre_low, grad_two, unit_one, inverse_one, w_attn_out, w_in, rows
-    )
-    inner_parts = weight_grad(
-        outer_sent[1], core_bit, normed_low, pre_low, FF // D, False, (attended, mixed_low)
-    )
-    inner_sum, inner_sent = reduce_panels(*inner_parts)
+        [], pre_low, grad_two, unit_one, inverse_one, w_attn_out, w_in, rows
+    )
+    inner_args = (normed_low, pre_low, FF // D, False, (attended, mixed_low))
+    inner_away = weight_half(8, outer_sent[1], 1 - core_bit, *inner_args)
+    inner_here = weight_half(60, [inner_away] + outer_sent[2], core_bit, *inner_args)
+    inner_sum, inner_sent, _ = reduce_panels(begin_sum(inner_away), inner_here)
     early, vec_early = unattend(
-        [inner_parts[0]] + outer_sent[2], 0, 2, q, k, v, p, grad_attended
-    )
-    late, vec_late = unattend(
-        [early] + outer_sent[3] + inner_sent[0], 1, 2, q, k, v, p, grad_attended
-    )
-    stack_low = jnp.concatenate([early, late])
+        outer_sent[3] + inner_sent[0], 0, 2, q, k, v, p, grad_attended
+    )
+    stack_low, vec_late = unattend([outer_sum], 1, 2, q, k, v, p, grad_attended, early)
+    project_args = (tokens, stack_low, 3, False)
+    project_away = weight_half(8, inner_sent[1], 1 - core_bit, *project_args)
+    project_here = weight_half(60, [project_away] + inner_sent[2], core_bit, *project_args)
     vec_heads = vec_early + vec_late
-    project_parts = weight_grad(
-        [outer_sum] + inner_sent[1], core_bit, tokens, stack_low, 3, False
-    )
-    project_sum, project_sent = reduce_panels(*project_parts)
-    grad_tokens = input_grad(
-        [project_parts[0]] + inner_sent[2], grad_one, stack_low, w_qkv
-    )
     grad_vector = jnp.concatenate(
         [
             jnp.stack([vec_one[0], vec_two[0], vec_one[1], vec_two[1]]),
@@ -807,11 +763,14 @@
             vec_inner[:, 0],
         ]
     )
-    vec_grad = grad_vector
-    for step in core + across + y_bits + z_bits:
-        vec_grad += swap(vec_grad, step)
+    project_sum, project_sent, vec_grad = reduce_panels(
+        begin_sum(project_away), project_here, grad_vector
+    )
+    grad_tokens = input_grad(
+        inner_sent[3] + project_sent[0], grad_one, stack_low, w_qkv
+    )
     parts = (project_sum, inner_sum[-1:], inner_sum[:-1], outer_sum)
-    gathered = spread(to_slots([grad_tokens, vec_grad], parts, owner_list))
+    gathered = spread(to_slots([grad_tokens], parts, owner_list))
     vec_grad = vec_grad.reshape(-1)
     new_master, new_first, new_second, master_copy = rotated_adam(
         row_place(), gathered, master, first_moment, second_moment, left_basis, right_basis

time: 318 us -> 279 us (0.88)
  waiting for transfers between devices: 97.9 us -> 65.1 us
  local copies, waits for them, and re-layouts: 17.6 us -> 9.56 us
  starting transfers between devices: 34.4 us -> 38.7 us
    ppermute x36 -> x32, waiting for transfers between devices: 97.9 us -> 65.1 us  [swap(): return lax.ppermute(send, step[0], [(i, i ^ step[1]) for i in range(size)])]
    squeeze x16 -> x1, local copies, waits for them, and re-layouts: 8.04 us -> 1.09 us  [pick(): return lax.dynamic_index_in_dim(array, index, dim, False)]
    pallas_call x1, Pallas kernels: 8.48 us -> 2.26 us  [to_slots(): pl.pallas_call(partial(slots_kernel, cols, len(after)), in_specs=[SMEM] +...]
    ppermute x36 -> x32, starting transfers between devices: 34.4 us -> 38.7 us  [swap(): return lax.ppermute(send, step[0], [(i, i ^ step[1]) for i in range(size)])]
    pallas_call x5 -> x8, Pallas kernels: 49.2 us -> 52.4 us  [the longest x6 36 us: weight_half(): pl.pallas_call(partial(weight_kernel, panels, len(after)), grid_spec=pltp...]
    convert_element_type x21 -> x20, other arithmetic: 10.8 us -> 11 us  [landed(): return (keep.astype(F32) + other.astype(F32)).astype(LOW)]
  transfers between devices with their start and end apart: 36 -> 32, of which waited for: 27 -> 21; matrix products, arithmetic and copies ran while one was open for 6% -> 4% of each run, Pallas kernels for 14% -> 27%
where the time goes in v1:
time: 279 us; the launch traced here: 278 us
  Pallas kernels  148 us (53%)
  waiting for transfers between devices  65.1 us (23%)
  starting transfers between devices  38.7 us (14%)
  other arithmetic  15.5 us (6%)
  local copies, waits for them, and re-layouts  9.56 us (3%)
    ppermute x32, waiting for transfers between devices, swap(): return lax.ppermute(send, step[0], [(i, i ^ step[1]) for i in range(size)])  65.1 us
    ppermute x32, starting transfers between devices, swap(): return lax.ppermute(send, step[0], [(i, i ^ step[1]) for i in range(size)])  38.7 us
    pallas_call x6, Pallas kernels, weight_half(): pl.pallas_call(partial(weight_kernel, panels, len(after)), grid_spec=pltp...  36 us
    pallas_call x1, Pallas kernels, feed(): pl.pallas_call(feed_kernel, grid=(total // TALL,), in_specs=[SMEM, SMEM,...  25.9 us
    pallas_call x1, Pallas kernels, rotated_adam(): pl.pallas_call(partial(adam_kernel, packed), grid_spec=pltpu.PrefetchScal...  19.6 us
    pallas_call x2, Pallas kernels, unattend(): pl.pallas_call(unattend_kernel, grid=(count,), in_specs=[ANY] * len(after...  16.3 us
    pallas_call x1, Pallas kernels, inner_grad(): pl.pallas_call(inner_kernel, grid=(total // TALL,), in_specs=[ANY] * len(...  12.4 us
    convert_element_type x20, other arithmetic, landed(): return (keep.astype(F32) + other.astype(F32)).astype(LOW)  11 us
  transfers between devices with their start and end apart: 32, of which 21 were waited for; matrix products, arithmetic and copies ran while one was open for 4% of the time, Pallas kernels for 27%

profile of v1, /device:TPU:0, one launch (start us, length us, event | category | flops | bytes accessed | tf_op | source)
XLA Modules:
  0.0 278.0 jit_solution(13875809737216638176)
XLA Ops:
  0.6 10.5 %attend.1 = (bf16[768,768]{1,0:T(8,128)(2,1)}, bf16[768,768]{1,0:T(8,128)(2,1)}, bf16[768,768]{1,0:T(8,128)(2,1)}, bf16[6,6,128,256]{3,2,1,0:T(8,128)(2,1)}, bf16[768,768]{1,0:T(8,128)(2,1)}) custom-call(bf16[768,768]{1,0:T(8,128)(2,1)} %refs_2_.3, bf16[3,768,768]{2,1,0:T(8,128)(2,1)} %refs_5_.3, f32[1,9216]{1,0:T(1,128)} %bitcast.229), custom_call_target="tpu_custom_call" | custom-call | flops 11000000512 | tf_op jit(solution)/shard_map/attend/pallas_call | solution.py:95
  11.2 25.9 %feed.1 = (bf16[768,768]{1,0:T(8,128)(2,1)}, bf16[768,3072]{1,0:T(8,128)(2,1)}, bf16[768,3072]{1,0:T(8,128)(2,1)}, bf16[768,768]{1,0:T(8,128)(2,1)}, bf16[768,76...) custom-call(s32[1]{0:T(128)} %bitcast.place, s32[32]{0:T(128)} %counts.3, ...), custom_call_target="tpu_custom_call" | custom-call | flops 28600000512 | tf_op jit(solution)/shard_map/feed/pallas_call | solution.py:168
  38.0 3.0 %collective-permute-start = (bf16[8,768]{1,0:T(8,128)(2,1)S(1)}, bf16[8,768]{1,0:T(8,128)(2,1)S(1)}, u32[]{:S(2)}, u32[]{:S(2)}) collective-permute-start(bf16[8,768]{1,0:T(8,128)(2,1)S(1)} %get-tuple-element.123), channel_id=1, source_target_pairs={{0,1},{1,0},{2,3},{3,2},{4,5},{5,4},{6,7},{7,6},{8,9},{9,8},{10,11... | collective-permute-start | bytes 36872 | tf_op jit(solution)/shard_map/ppermute | solution.py:576
  46.6 3.0 %collective-permute-start.2 = (bf16[32,768]{1,0:T(8,128)(2,1)S(1)}, bf16[32,768]{1,0:T(8,128)(2,1)S(1)}, u32[]{:S(2)}, u32[]{:S(2)}) collective-permute-start(bf16[32,768]{1,0:T(8,128)(2,1)S(1)} %pad_maximum_fusion.8), channel_id=1, source_target_pairs={{0,4},{1,5},{2,6},{3,7},{4,0},{5,1},{6,2},{7,3},{8,12},{9,13},{10,... | collective-permute-start | bytes 147464 | tf_op jit(solution)/shard_map/ppermute | solution.py:576
  55.5 4.7 %collective-permute-done.4 = bf16[128,768]{1,0:T(8,128)(2,1)S(1)} collective-permute-done((bf16[128,768]{1,0:T(8,128)(2,1)S(1)}, bf16[128,768]{1,0:T(8,128)(2,1)S(1)}, u32[]{:S(2)}, u32[]{:S(2)}) %collective-permute-start.4) | collective-permute-done | bytes 196640 | tf_op jit(solution)/shard_map/ppermute | solution.py:576
  60.9 2.7 contrast.1
  63.6 5.1 %outer.1 = (f32[768,768]{1,0:T(8,128)}, bf16[768,768]{1,0:T(8,128)(2,1)}, f32[3,768]{1,0:T(4,128)}) custom-call(s32[1]{0:T(128)} %bitcast.place, s32[32]{0:T(128)} %counts.3, bf16[768,768]{1,0:T(8,128)(2,1)} %out_grad.1, f32[8,768]{1,0:T(8,128)} %get-tuple-element.45.grad_cls, bf16[768,768]{1,0:T(8,128)(2,1)} %get-tuple-element.46.unit_two, ...), custom_call_target="tpu_custom_call" | custom-call | flops 5500000256 | tf_op jit(solution)/shard_map/outer/pallas_call | solution.py:214
  68.7 5.6 %weight.6.refs_0_ = bf16[4,384,768]{2,1,0:T(8,128)(2,1)} custom-call(s32[1]{0:T(128)} %bitcast.3.side, bf16[768,3072]{1,0:T(8,128)(2,1)} %get-tuple-element.44.refs_0_.refs_1_, bf16[768,768]{1,0:T(8,128)(2,1)} %get-tuple-element.48.refs_1_.refs_2_), custom_call_target="tpu_custom_call" | custom-call | flops 8800000000 | tf_op jit(solution)/shard_map/weight/pallas_call | solution.py:251
  74.4 5.8 %weight.7 = bf16[4,384,768]{2,1,0:T(8,128)(2,1)} custom-call(s32[1]{0:T(128)} %bitcast.2.side, bf16[4,384,768]{2,1,0:T(8,128)(2,1)} %weight.6.refs_0_, bf16[768,3072]{1,0:T(8,128)(2,1)} %get-tuple-element.44.refs_0_.refs_1_, bf16[768,768]{1,0:T(8,128)(2,1)} %get-tuple-element.48.refs_1_.refs_2_), custom_call_target="tpu_custom_call" | custom-call | flops 65999998976 | tf_op jit(solution)/shard_map/weight/pallas_call | solution.py:251
  86.5 9.1 %slope.1 = (bf16[768,3072]{1,0:T(8,128)(2,1)}, f32[4,1,768]{2,1,0:T(1,128)}) custom-call(bf16[768,384]{1,0:T(8,128)(2,1)} %bitcast.192, bf16[768,384]{1,0:T(8,128)(2,1)} %bitcast.194, bf16[768,768]{1,0:T(8,128)(2,1)} %get-tuple-element.48.refs_1_.refs_2_, bf16[768,3072]{1,0:T(8,128)(2,1)} %get-tuple-element.50.refs_3_, bf16[3072,768]{1,0:T(8,128)(2,1)} %refs_4_.2), custom_call_target="tpu_custom_call" | custom-call | flops 9900000256 | tf_op jit(solution)/shard_map/slope/pallas_call | solution.py:281
  95.6 3.0 %collective-permute-done.7 = bf16[768,384]{1,0:T(8,128)(2,1)S(1)} collective-permute-done((bf16[768,384]{1,0:T(8,128)(2,1)S(1)}, bf16[768,384]{1,0:T(8,128)(2,1)S(1)}, u32[]{:S(2)}, u32[]{:S(2)}) %collective-permute-start.7) | collective-permute-done | bytes 589856 | tf_op jit(solution)/shard_map/ppermute | solution.py:576
  102.5 12.4 %inner.1 = (f32[768,768]{1,0:T(8,128)}, bf16[768,768]{1,0:T(8,128)(2,1)}, bf16[768,768]{1,0:T(8,128)(2,1)}, f32[3,768]{1,0:T(4,128)}) custom-call(bf16[768,3072]{1,0:T(8,128)(2,1)} %get-tuple-element.51.refs_0_.refs_3_, f32[768,768]{1,0:T(8,128)} %get-tuple-element.52.refs_1_, bf16[768,768]{1,0:T(8,128)(2,1)} %get-tuple-element.53.refs_2_, ...), custom_call_target="tpu_custom_call" | custom-call | flops 13200000000 | tf_op jit(solution)/shard_map/inner/pallas_call | solution.py:321
  117.7 7.2 %weight.8.refs_0_ = bf16[5,384,768]{2,1,0:T(8,128)(2,1)} custom-call(s32[1]{0:T(128)} %bitcast.3.side, bf16[384,384]{1,0:T(8,128)(2,1)} %bitcast.213, bf16[384,384]{1,0:T(8,128)(2,1)} %bitcast.211, bf16[768,768]{1,0:T(8,128)(2,1)} %get-tuple-element.49.refs_2_, bf16[768,3072]{1,0:T(8,128)(2,1)} %get-tuple-element.51.refs_0_.refs_3_, ...), custom_call_target="tpu_custom_call" | custom-call | flops 8800000000 | tf_op jit(solution)/shard_map/weight/pallas_call | solution.py:251
  125.0 3.1 %collective-permute-start.17 = (bf16[96,768]{1,0:T(8,128)(2,1)S(1)}, bf16[96,768]{1,0:T(8,128)(2,1)S(1)}, u32[]{:S(2)}, u32[]{:S(2)}) collective-permute-start(bf16[96,768]{1,0:T(8,128)(2,1)S(1)} %bitcast.224), channel_id=1, source_target_pairs={{0,4},{1,5},{2,6},{3,7},{4,0},{5,1},{6,2},{7,3},{8,12},{9,13},{10,... | collective-permute-start | bytes 442376 | tf_op jit(solution)/shard_map/ppermute | solution.py:576
  128.1 7.1 %weight.9 = bf16[5,384,768]{2,1,0:T(8,128)(2,1)} custom-call(s32[1]{0:T(128)} %bitcast.2.side, bf16[5,384,768]{2,1,0:T(8,128)(2,1)} %weight.8.refs_0_, bf16[192,768]{1,0:T(8,128)(2,1)} %bitcast.215, bf16[768,768]{1,0:T(8,128)(2,1)} %get-tuple-element.49.refs_2_, bf16[768,3072]{1,0:T(8,128)(2,1)} %get-tuple-element.51.refs_0_.refs_3_, ...), custom_call_target="tpu_custom_call" | custom-call | flops 65999998976 | tf_op jit(solution)/shard_map/weight/pallas_call | solution.py:251
  136.0 2.7 add_convert_fusion
  142.0 8.2 %unattend.2 = (bf16[768,2304]{1,0:T(8,128)(2,1)}, f32[2,768]{1,0:T(2,128)}) custom-call(bf16[96,768]{1,0:T(8,128)(2,1)} %bitcast.225, bf16[960,384]{1,0:T(8,128)(2,1)} %bitcast.187, bf16[960,384]{1,0:T(8,128)(2,1)} %bitcast.30.refs_2_, bf16[768,768]{1,0:T(8,128)(2,1)} %get-tuple-element.56.refs_3_.refs_2_, ...), custom_call_target="tpu_custom_call" | custom-call | flops 8800000000 | tf_op jit(solution)/shard_map/unattend/pallas_call | solution.py:379
  150.2 8.2 %unattend.3 = (bf16[768,2304]{1,0:T(8,128)(2,1)}, f32[2,768]{1,0:T(2,128)}) custom-call(bf16[768,2304]{1,0:T(8,128)(2,1)} %get-tuple-element.61.refs_0_, bf16[4,24,768]{2,1,0:T(8,128)(2,1)} %fusion.22.refs_1_.refs_4_, bf16[768,768]{1,0:T(8,128)(2,1)} %get-tuple-element.56.refs_3_.refs_2_, ...), custom_call_target="tpu_custom_call", output_to_operand_aliasing={{0}: (0, {})} | custom-call | flops 8800000000 | tf_op jit(solution)/shard_map/unattend/pallas_call | solution.py:379
  165.0 5.1 %weight.10.refs_0_ = bf16[3,384,768]{2,1,0:T(8,128)(2,1)} custom-call(s32[1]{0:T(128)} %bitcast.3.side, bf16[480,384]{1,0:T(8,128)(2,1)} %bitcast.207, bf16[480,384]{1,0:T(8,128)(2,1)} %bitcast.205, bf16[768,768]{1,0:T(8,128)(2,1)} %refs_2_.3, bf16[768,2304]{1,0:T(8,128)(2,1)} %get-tuple-element.62.refs_3_.refs_4_), custom_call_target="tpu_custom_call" | custom-call | flops 8800000000 | tf_op jit(solution)/shard_map/weight/pallas_call | solution.py:251
  170.1 3.1 %collective-permute-done.14 = bf16[480,384]{1,0:T(8,128)(2,1)S(1)} collective-permute-done((bf16[480,384]{1,0:T(8,128)(2,1)S(1)}, bf16[480,384]{1,0:T(8,128)(2,1)S(1)}, u32[]{:S(2)}, u32[]{:S(2)}) %collective-permute-start.14) | collective-permute-done | bytes 368672 | tf_op jit(solution)/shard_map/ppermute | solution.py:576
  174.8 5.1 %weight.11 = bf16[3,384,768]{2,1,0:T(8,128)(2,1)} custom-call(s32[1]{0:T(128)} %bitcast.2.side, bf16[3,384,768]{2,1,0:T(8,128)(2,1)} %weight.10.refs_0_, bf16[240,768]{1,0:T(8,128)(2,1)} %bitcast.202, bf16[768,768]{1,0:T(8,128)(2,1)} %refs_2_.3, bf16[768,2304]{1,0:T(8,128)(2,1)} %get-tuple-element.62.refs_3_.refs_4_), custom_call_target="tpu_custom_call" | custom-call | flops 65999998976 | tf_op jit(solution)/shard_map/weight/pallas_call | solution.py:251
  185.2 4.2 %collective-permute-done.15 = bf16[240,768]{1,0:T(8,128)(2,1)S(1)} collective-permute-done((bf16[240,768]{1,0:T(8,128)(2,1)S(1)}, bf16[240,768]{1,0:T(8,128)(2,1)S(1)}, u32[]{:S(2)}, u32[]{:S(2)}) %collective-permute-start.15) | collective-permute-done | bytes 368672 | tf_op jit(solution)/shard_map/ppermute | solution.py:576
  189.6 4.2 %collective-permute-done.22 = bf16[576,384]{1,0:T(8,128)(2,1)S(1)} collective-permute-done((bf16[576,384]{1,0:T(8,128)(2,1)S(1)}, bf16[576,384]{1,0:T(8,128)(2,1)S(1)}, u32[]{:S(2)}, u32[]{:S(2)}) %collective-permute-start.22) | collective-permute-done | bytes 442400 | tf_op jit(solution)/shard_map/ppermute | solution.py:576
  200.4 2.9 %collective-permute-done.21 = bf16[312,384]{1,0:T(8,128)(2,1)S(1)} collective-permute-done((bf16[312,384]{1,0:T(8,128)(2,1)S(1)}, bf16[312,384]{1,0:T(8,128)(2,1)S(1)}, u32[]{:S(2)}, u32[]{:S(2)}) %collective-permute-start.21) | collective-permute-done | bytes 239648 | tf_op jit(solution)/shard_map/ppermute | solution.py:576
  207.1 2.7 collective-permute-done.24
  209.9 3.6 %collective-permute-start.25 = (bf16[84,768]{1,0:T(8,128)(2,1)S(1)}, bf16[84,768]{1,0:T(8,128)(2,1)S(1)}, u32[]{:S(2)}, u32[]{:S(2)}) collective-permute-start(bf16[84,768]{1,0:T(8,128)(2,1)S(1)} %pad_maximum_fusion.6), channel_id=1, source_target_pairs={{0,4},{1,5},{2,6},{3,7},{4,0},{5,1},{6,2},{7,3},{8,12},{9,13},{10,... | collective-permute-start | bytes 387080 | tf_op jit(solution)/shard_map/ppermute | solution.py:576
  213.6 7.8 %input.1.refs_0_ = f32[768,768]{1,0:T(8,128)} custom-call(bf16[120,768]{1,0:T(8,128)(2,1)} %bitcast.223, bf16[600,384]{1,0:T(8,128)(2,1)} %copy-done.3, bf16[576,384]{1,0:T(8,128)(2,1)} %bitcast.196, f32[768,768]{1,0:T(8,128)} %get-tuple-element.68.refs_3_, bf16[768,2304]{1,0:T(8,128)(2,1)} %get-tuple-element.62.refs_3_.refs_4_, bf16[3,768,768]{2,1,0:T(8,128)(2,1)} %refs_5_.3), custom_call_target="tpu_custom_call" | custom-call | flops 8800000000 | tf_op jit(solution)/shard_map/input/pallas_call | solution.py:411
  225.5 8.3 %collective-permute-done.27 = bf16[1,2,2,72,384]{4,3,0,2,1:T(8,128)(2,1)S(1)} collective-permute-done((bf16[1,2,2,72,384]{4,3,0,2,1:T(8,128)(2,1)S(1)}, bf16[1,2,2,72,384]{4,3,0,2,1:T(8,128)(2,1)S(1)}, u32[]{:S(2)}, u32[]{:S(2)}) %collective-permute-start.27) | collective-permute-done | bytes 221216 | tf_op jit(solution)/shard_map/ppermute | solution.py:576
  233.9 5.9 %collective-permute-done.28 = bf16[2,2,72,384]{3,2,0,1:T(8,128)(2,1)S(1)} collective-permute-done((bf16[2,2,72,384]{3,2,0,1:T(8,128)(2,1)S(1)}, bf16[2,2,72,384]{3,2,0,1:T(8,128)(2,1)S(1)}, u32[]{:S(2)}, u32[]{:S(2)}) %collective-permute-start.28) | collective-permute-done | bytes 221216 | tf_op jit(solution)/shard_map/ppermute | solution.py:576
  240.5 5.3 %collective-permute-done.29 = bf16[4,72,384]{2,1,0:T(8,128)(2,1)S(1)} collective-permute-done((bf16[4,72,384]{2,1,0:T(8,128)(2,1)S(1)}, bf16[4,72,384]{2,1,0:T(8,128)(2,1)S(1)}, u32[]{:S(2)}, u32[]{:S(2)}) %collective-permute-start.29) | collective-permute-done | bytes 221216 | tf_op jit(solution)/shard_map/ppermute | solution.py:576
  246.2 8.1 %collective-permute-done.30 = bf16[8,72,384]{2,1,0:T(8,128)(2,1)S(1)} collective-permute-done((bf16[8,72,384]{2,1,0:T(8,128)(2,1)S(1)}, bf16[8,72,384]{2,1,0:T(8,128)(2,1)S(1)}, u32[]{:S(2)}, u32[]{:S(2)}) %collective-permute-start.30) | collective-permute-done | bytes 442400 | tf_op jit(solution)/shard_map/ppermute | solution.py:576
  258.3 19.6 %adam.1 = (f32[6,192,768]{2,1,0:T(8,128)}, f32[6,192,768]{2,1,0:T(8,128)}, f32[6,192,768]{2,1,0:T(8,128)}, bf16[6,192,768]{2,1,0:T(8,128)(2,1)}) custom-call(s32[1]{0:T(128)} %bitcast.48.position, bf16[32,72,384]{2,1,0:T(8,128)(2,1)} %pad_maximum_fusion.gathered, f32[6,192,768]{2,1,0:T(8,128)} %bitcast.235, f32[6,192,768]{2,1,0:T(8,128)} %bitcast.236, ...), custom_call_target="tpu_custom_call" | custom-call | flops 22000001024 | tf_op jit(solution)/shard_map/adam/pallas_call | solution.py:548
  (190 shorter events, 63.2 us)
Async XLA Ops:
  38.0 4.7 %collective-permute-start = (bf16[8,768]{1,0:T(8,128)(2,1)S(1)}, bf16[8,768]{1,0:T(8,128)(2,1)S(1)}, u32[]{:S(2)}, u32[]{:S(2)}) collective-permute-start(bf16[8,768]{1,0:T(8,128)(2,1)S(1)} %get-tuple-element.123), channel_id=1, source_target_pairs={{0,1},{1,0},{2,3},{3,2},{4,5},{5,4},{6,7},{7,6},{8,9},{9,8},{10,11... | collective-permute-start | bytes 36872 | tf_op jit(solution)/shard_map/ppermute | solution.py:576
  42.7 3.9 %collective-permute-start.1 = (bf16[16,768]{1,0:T(8,128)(2,1)S(1)}, bf16[16,768]{1,0:T(8,128)(2,1)S(1)}, u32[]{:S(2)}, u32[]{:S(2)}) collective-permute-start(bf16[16,768]{1,0:T(8,128)(2,1)S(1)} %pad_maximum_fusion.9), channel_id=1, source_target_pairs={{0,2},{1,3},{2,0},{3,1},{4,6},{5,7},{6,4},{7,5},{8,10},{9,11},{10,... | collective-permute-start | bytes 73736 | tf_op jit(solution)/shard_map/ppermute | solution.py:576
  46.6 5.1 %collective-permute-start.2 = (bf16[32,768]{1,0:T(8,128)(2,1)S(1)}, bf16[32,768]{1,0:T(8,128)(2,1)S(1)}, u32[]{:S(2)}, u32[]{:S(2)}) collective-permute-start(bf16[32,768]{1,0:T(8,128)(2,1)S(1)} %pad_maximum_fusion.8), channel_id=1, source_target_pairs={{0,4},{1,5},{2,6},{3,7},{4,0},{5,1},{6,2},{7,3},{8,12},{9,13},{10,... | collective-permute-start | bytes 147464 | tf_op jit(solution)/shard_map/ppermute | solution.py:576
  51.7 1.4 collective-permute-start.3
  53.1 7.1 %collective-permute-start.4 = (bf16[128,768]{1,0:T(8,128)(2,1)S(1)}, bf16[128,768]{1,0:T(8,128)(2,1)S(1)}, u32[]{:S(2)}, u32[]{:S(2)}) collective-permute-start(bf16[128,768]{1,0:T(8,128)(2,1)S(1)} %get-tuple-element.107), channel_id=1, source_target_pairs={{0,16},{8,24},{16,0},{24,8},{1,17},{9,25},{17,1},{25,9},{2,18},{10... | collective-permute-start | bytes 589832 | tf_op jit(solution)/shard_map/ppermute | solution.py:576
  74.4 5.9 %collective-permute-start.5 = (bf16[4,384,768]{2,1,0:T(8,128)(2,1)}, bf16[4,384,768]{2,1,0:T(8,128)(2,1)S(1)}, u32[]{:S(2)}, u32[]{:S(2)}) collective-permute-start(bf16[4,384,768]{2,1,0:T(8,128)(2,1)} %weight.6.refs_0_), channel_id=1, source_target_pairs={{0,8},{8,0},{16,24},{24,16},{1,9},{9,1},{17,25},{25,17},{2,10},{10... | collective-permute-start | bytes 7077896 | tf_op jit(solution)/shard_map/ppermute | solution.py:576
  83.0 15.6 %collective-permute-start.7 = (bf16[768,384]{1,0:T(8,128)(2,1)S(1)}, bf16[768,384]{1,0:T(8,128)(2,1)S(1)}, u32[]{:S(2)}, u32[]{:S(2)}) collective-permute-start(bf16[768,384]{1,0:T(8,128)(2,1)S(1)} %bitcast.193), channel_id=1, source_target_pairs={{0,1},{1,0},{2,3},{3,2},{4,5},{5,4},{6,7},{7,6},{8,9},{9,8},{10,11... | collective-permute-start | bytes 1769480 | tf_op jit(solution)/shard_map/ppermute | solution.py:576
  85.0 15.7 %collective-permute-start.6 = (bf16[768,384]{1,0:T(8,128)(2,1)S(1)}, bf16[768,384]{1,0:T(8,128)(2,1)S(1)}, u32[]{:S(2)}, u32[]{:S(2)}) collective-permute-start(bf16[768,384]{1,0:T(8,128)(2,1)S(1)} %bitcast.191), channel_id=1, source_target_pairs={{0,16},{8,24},{16,0},{24,8},{1,17},{9,25},{17,1},{25,9},{2,18},{10... | collective-permute-start | bytes 1769480 | tf_op jit(solution)/shard_map/ppermute | solution.py:576
  98.9 16.9 %collective-permute-start.9 = (bf16[384,384]{1,0:T(8,128)(2,1)S(1)}, bf16[384,384]{1,0:T(8,128)(2,1)S(1)}, u32[]{:S(2)}, u32[]{:S(2)}) collective-permute-start(bf16[384,384]{1,0:T(8,128)(2,1)S(1)} %bitcast.210), channel_id=1, source_target_pairs={{0,16},{8,24},{16,0},{24,8},{1,17},{9,25},{17,1},{25,9},{2,18},{10... | collective-permute-start | bytes 884744 | tf_op jit(solution)/shard_map/ppermute | solution.py:576
  100.9 14.9 %collective-permute-start.8 = (bf16[384,384]{1,0:T(8,128)(2,1)S(1)}, bf16[384,384]{1,0:T(8,128)(2,1)S(1)}, u32[]{:S(2)}, u32[]{:S(2)}) collective-permute-start(bf16[384,384]{1,0:T(8,128)(2,1)S(1)} %bitcast.212), channel_id=1, source_target_pairs={{0,1},{1,0},{2,3},{3,2},{4,5},{5,4},{6,7},{7,6},{8,9},{9,8},{10,11... | collective-permute-start | bytes 884744 | tf_op jit(solution)/shard_map/ppermute | solution.py:576
  116.1 8.8 %collective-permute-start.16 = (bf16[192,768]{1,0:T(8,128)(2,1)S(1)}, bf16[192,768]{1,0:T(8,128)(2,1)S(1)}, u32[]{:S(2)}, u32[]{:S(2)}) collective-permute-start(bf16[192,768]{1,0:T(8,128)(2,1)S(1)} %bitcast.214), channel_id=1, source_target_pairs={{0,2},{1,3},{2,0},{3,1},{4,6},{5,7},{6,4},{7,5},{8,10},{9,11},{10,... | collective-permute-start | bytes 884744 | tf_op jit(solution)/shard_map/ppermute | solution.py:576
  124.9 11.1 %collective-permute-start.10 = (bf16[5,384,768]{2,1,0:T(8,128)(2,1)}, bf16[5,384,768]{2,1,0:T(8,128)(2,1)S(1)}, u32[]{:S(2)}, u32[]{:S(2)}) collective-permute-start(bf16[5,384,768]{2,1,0:T(8,128)(2,1)} %weight.8.refs_0_), channel_id=1, source_target_pairs={{0,8},{8,0},{16,24},{24,16},{1,9},{9,1},{17,25},{25,17},{2,10},{10... | collective-permute-start | bytes 8847368 | tf_op jit(solution)/shard_map/ppermute | solution.py:576
  125.0 10.3 %collective-permute-start.17 = (bf16[96,768]{1,0:T(8,128)(2,1)S(1)}, bf16[96,768]{1,0:T(8,128)(2,1)S(1)}, u32[]{:S(2)}, u32[]{:S(2)}) collective-permute-start(bf16[96,768]{1,0:T(8,128)(2,1)S(1)} %bitcast.224), channel_id=1, source_target_pairs={{0,4},{1,5},{2,6},{3,7},{4,0},{5,1},{6,2},{7,3},{8,12},{9,13},{10,... | collective-permute-start | bytes 442376 | tf_op jit(solution)/shard_map/ppermute | solution.py:576
  140.3 20.1 %collective-permute-start.13 = (bf16[960,384]{1,0:T(8,128)(2,1)}, bf16[960,384]{1,0:T(8,128)(2,1)}, u32[]{:S(2)}, u32[]{:S(2)}) collective-permute-start(bf16[960,384]{1,0:T(8,128)(2,1)} %bitcast.30.refs_2_), channel_id=1, source_target_pairs={{0,1},{1,0},{2,3},{3,2},{4,5},{5,4},{6,7},{7,6},{8,9},{9,8},{10,11... | collective-permute-start | bytes 2211848 | tf_op jit(solution)/shard_map/ppermute | solution.py:576
  140.9 21.0 %collective-permute-start.11 = (bf16[960,384]{1,0:T(8,128)(2,1)S(1)}, bf16[960,384]{1,0:T(8,128)(2,1)S(1)}, u32[]{:S(2)}, u32[]{:S(2)}) collective-permute-start(bf16[960,384]{1,0:T(8,128)(2,1)S(1)} %bitcast.186), channel_id=1, source_target_pairs={{0,16},{8,24},{16,0},{24,8},{1,17},{9,25},{17,1},{25,9},{2,18},{10... | collective-permute-start | bytes 2211848 | tf_op jit(solution)/shard_map/ppermute | solution.py:576
  159.1 1.3 collective-permute-start.19
  162.6 10.7 %collective-permute-start.14 = (bf16[480,384]{1,0:T(8,128)(2,1)S(1)}, bf16[480,384]{1,0:T(8,128)(2,1)S(1)}, u32[]{:S(2)}, u32[]{:S(2)}) collective-permute-start(bf16[480,384]{1,0:T(8,128)(2,1)S(1)} %bitcast.204), channel_id=1, source_target_pairs={{0,16},{8,24},{16,0},{24,8},{1,17},{9,25},{17,1},{25,9},{2,18},{10... | collective-permute-start | bytes 1105928 | tf_op jit(solution)/shard_map/ppermute | solution.py:576
  163.5 10.4 %collective-permute-start.12 = (bf16[480,384]{1,0:T(8,128)(2,1)S(1)}, bf16[480,384]{1,0:T(8,128)(2,1)S(1)}, u32[]{:S(2)}, u32[]{:S(2)}) collective-permute-start(bf16[480,384]{1,0:T(8,128)(2,1)S(1)} %bitcast.206), channel_id=1, source_target_pairs={{0,1},{1,0},{2,3},{3,2},{4,5},{5,4},{6,7},{7,6},{8,9},{9,8},{10,11... | collective-permute-start | bytes 1105928 | tf_op jit(solution)/shard_map/ppermute | solution.py:576
  170.1 10.5 %collective-permute-start.18 = (bf16[3,384,768]{2,1,0:T(8,128)(2,1)}, bf16[3,384,768]{2,1,0:T(8,128)(2,1)S(1)}, u32[]{:S(2)}, u32[]{:S(2)}) collective-permute-start(bf16[3,384,768]{2,1,0:T(8,128)(2,1)} %weight.10.refs_0_), channel_id=1, source_target_pairs={{0,8},{8,0},{16,24},{24,16},{1,9},{9,1},{17,25},{25,17},{2,10},{10... | collective-permute-start | bytes 5308424 | tf_op jit(solution)/shard_map/ppermute | solution.py:576
  179.9 9.5 %collective-permute-start.15 = (bf16[240,768]{1,0:T(8,128)(2,1)S(1)}, bf16[240,768]{1,0:T(8,128)(2,1)S(1)}, u32[]{:S(2)}, u32[]{:S(2)}) collective-permute-start(bf16[240,768]{1,0:T(8,128)(2,1)S(1)} %bitcast.203), channel_id=1, source_target_pairs={{0,2},{1,3},{2,0},{3,1},{4,6},{5,7},{6,4},{7,5},{8,10},{9,11},{10,... | collective-permute-start | bytes 1105928 | tf_op jit(solution)/shard_map/ppermute | solution.py:576
  182.9 10.9 %collective-permute-start.22 = (bf16[576,384]{1,0:T(8,128)(2,1)S(1)}, bf16[576,384]{1,0:T(8,128)(2,1)S(1)}, u32[]{:S(2)}, u32[]{:S(2)}) collective-permute-start(bf16[576,384]{1,0:T(8,128)(2,1)S(1)} %bitcast.195), channel_id=1, source_target_pairs={{0,1},{1,0},{2,3},{3,2},{4,5},{5,4},{6,7},{7,6},{8,9},{9,8},{10,11... | collective-permute-start | bytes 1327112 | tf_op jit(solution)/shard_map/ppermute | solution.py:576
  184.6 12.1 %collective-permute-start.20 = (bf16[600,384]{1,0:T(8,128)(2,1)S(1)}, bf16[600,384]{1,0:T(8,128)(2,1)S(1)}, u32[]{:S(2)}, u32[]{:S(2)}) collective-permute-start(bf16[600,384]{1,0:T(8,128)(2,1)S(1)} %pad_maximum_fusion.2.refs_1_), channel_id=1, source_target_pairs={{0,16},{8,24},{16,0},{24,8},{1,17},{9,25},{17,1},{25,9},{2,18},{10... | collective-permute-start | bytes 1382408 | tf_op jit(solution)/shard_map/ppermute | solution.py:576
  193.9 6.4 %collective-permute-start.23 = (bf16[288,384]{1,0:T(8,128)(2,1)S(1)}, bf16[288,384]{1,0:T(8,128)(2,1)S(1)}, u32[]{:S(2)}, u32[]{:S(2)}) collective-permute-start(bf16[288,384]{1,0:T(8,128)(2,1)S(1)} %bitcast.220), channel_id=1, source_target_pairs={{0,16},{8,24},{16,0},{24,8},{1,17},{9,25},{17,1},{25,9},{2,18},{10... | collective-permute-start | bytes 663560 | tf_op jit(solution)/shard_map/ppermute | solution.py:576
  197.1 6.2 %collective-permute-start.21 = (bf16[312,384]{1,0:T(8,128)(2,1)S(1)}, bf16[312,384]{1,0:T(8,128)(2,1)S(1)}, u32[]{:S(2)}, u32[]{:S(2)}) collective-permute-start(bf16[312,384]{1,0:T(8,128)(2,1)S(1)} %pad_maximum_fusion.5), channel_id=1, source_target_pairs={{0,1},{1,0},{2,3},{3,2},{4,5},{5,4},{6,7},{7,6},{8,9},{9,8},{10,11... | collective-permute-start | bytes 718856 | tf_op jit(solution)/shard_map/ppermute | solution.py:576
  197.2 8.6 %collective-permute-start.26 = (bf16[120,768]{1,0:T(8,128)(2,1)S(1)}, bf16[120,768]{1,0:T(8,128)(2,1)S(1)}, u32[]{:S(2)}, u32[]{:S(2)}) collective-permute-start(bf16[120,768]{1,0:T(8,128)(2,1)S(1)} %bitcast.222), channel_id=1, source_target_pairs={{0,4},{1,5},{2,6},{3,7},{4,0},{5,1},{6,2},{7,3},{8,12},{9,13},{10,... | collective-permute-start | bytes 552968 | tf_op jit(solution)/shard_map/ppermute | solution.py:576
  203.5 6.3 %collective-permute-start.24 = (bf16[156,768]{1,0:T(8,128)(2,1)S(1)}, bf16[156,768]{1,0:T(8,128)(2,1)S(1)}, u32[]{:S(2)}, u32[]{:S(2)}) collective-permute-start(bf16[156,768]{1,0:T(8,128)(2,1)S(1)} %pad_maximum_fusion.4), channel_id=1, source_target_pairs={{0,2},{1,3},{2,0},{3,1},{4,6},{5,7},{6,4},{7,5},{8,10},{9,11},{10,... | collective-permute-start | bytes 718856 | tf_op jit(solution)/shard_map/ppermute | solution.py:576
  209.9 11.4 %collective-permute-start.25 = (bf16[84,768]{1,0:T(8,128)(2,1)S(1)}, bf16[84,768]{1,0:T(8,128)(2,1)S(1)}, u32[]{:S(2)}, u32[]{:S(2)}) collective-permute-start(bf16[84,768]{1,0:T(8,128)(2,1)S(1)} %pad_maximum_fusion.6), channel_id=1, source_target_pairs={{0,4},{1,5},{2,6},{3,7},{4,0},{5,1},{6,2},{7,3},{8,12},{9,13},{10,... | collective-permute-start | bytes 387080 | tf_op jit(solution)/shard_map/ppermute | solution.py:576
  225.4 8.4 %collective-permute-start.27 = (bf16[1,2,2,72,384]{4,3,0,2,1:T(8,128)(2,1)S(1)}, bf16[1,2,2,72,384]{4,3,0,2,1:T(8,128)(2,1)S(1)}, u32[]{:S(2)}, u32[]{:S(2)}) collective-permute-start(bf16[1,2,2,72,384]{4,3,0,2,1:T(8,128)(2,1)S(1)} %get-tuple-element.105), channel_id=1, source_target_pairs={{0,4},{1,5},{2,6},{3,7},{4,0},{5,1},{6,2},{7,3},{8,12},{9,13},{10,... | collective-permute-start | bytes 663560 | tf_op jit(solution)/shard_map/ppermute | solution.py:576
  233.8 6.0 %collective-permute-start.28 = (bf16[2,2,72,384]{3,2,0,1:T(8,128)(2,1)S(1)}, bf16[2,2,72,384]{3,2,0,1:T(8,128)(2,1)S(1)}, u32[]{:S(2)}, u32[]{:S(2)}) collective-permute-start(bf16[2,2,72,384]{3,2,0,1:T(8,128)(2,1)S(1)} %get-tuple-element.103), channel_id=1, source_target_pairs={{0,2},{1,3},{2,0},{3,1},{4,6},{5,7},{6,4},{7,5},{8,10},{9,11},{10,... | collective-permute-start | bytes 663560 | tf_op jit(solution)/shard_map/ppermute | solution.py:576
  239.9 6.0 %collective-permute-start.29 = (bf16[4,72,384]{2,1,0:T(8,128)(2,1)S(1)}, bf16[4,72,384]{2,1,0:T(8,128)(2,1)S(1)}, u32[]{:S(2)}, u32[]{:S(2)}) collective-permute-start(bf16[4,72,384]{2,1,0:T(8,128)(2,1)S(1)} %get-tuple-element.102), channel_id=1, source_target_pairs={{0,1},{1,0},{2,3},{3,2},{4,5},{5,4},{6,7},{7,6},{8,9},{9,8},{10,11... | collective-permute-start | bytes 663560 | tf_op jit(solution)/shard_map/ppermute | solution.py:576
  245.9 8.4 %collective-permute-start.30 = (bf16[8,72,384]{2,1,0:T(8,128)(2,1)S(1)}, bf16[8,72,384]{2,1,0:T(8,128)(2,1)S(1)}, u32[]{:S(2)}, u32[]{:S(2)}) collective-permute-start(bf16[8,72,384]{2,1,0:T(8,128)(2,1)S(1)} %pad_maximum_fusion.3), channel_id=1, source_target_pairs={{0,16},{8,24},{16,0},{24,8},{1,17},{9,25},{17,1},{25,9},{2,18},{10... | collective-permute-start | bytes 1327112 | tf_op jit(solution)/shard_map/ppermute | solution.py:576
  254.4 2.5 collective-permute-start.31
  (22 other events, 232.1 us)
